TPU v7x, 32 devices: a whole 2x2x4 slice. The times are simulated.
32 devices in a mesh: seq: 8 (over y, x, core), head: 4 (over z).
Axes of the slice: x: 2, y: 2, z: 4, core: 2. Of those that a mesh axis runs over, the one named last changes fastest.
Arguments:
- queries: bfloat16 [512, 8192], P('seq', 'head'), may hold values from -6 to 6
- keys: bfloat16 [512, 1024], P('seq'), may hold values from -6 to 6
- values: bfloat16 [512, 1024], P('seq'), may hold values from -6 to 6
- vertical: int32 [64, 8], replicated, may hold values from -1 to 7, as said below
- slash: int32 [64, 8], replicated, may hold values from -1 to 7, as said below
- plan: int32 [64], replicated, may hold values from 0 to 63, each once
Outputs:
- attended: bfloat16 [512, 8192], P('seq', 'head')
Inputs may be any that keep to these rules, and one draw needn't show every extreme that they name: `vertical`: entries of 0 or more name key blocks of 64 positions; -1 marks an unused entry, and every row has at least one used entry. `slash`: entries of 0 or more are offsets back from a query's own block; -1 marks an unused entry; the first entry of every row is 0. `plan`: A permutation of the query heads.
All inputs are finite; a program needn't handle non-finite values.
Results may differ from a plain program's by a relative error of at most 0.0044.
Values may be sent and summed in bfloat16 or wider, within the bound.
No kernel may reach another device: no remote copies, remote signals or barrier semaphores. Data moves between devices by JAX's collectives and lax.ppermute only.
A program may use at most 64 MiB of HBM per device.

v0:
```python
import jax
import jax.numpy as jnp
from jax import lax
from jax.sharding import PartitionSpec as P

HD = 128
QH = 64
KVH = 8
BLK = 64


floor_value = -1e30


def block_mask(query_blocks, key_blocks, vertical_rows, slash_rows, query_pos, key_pos):
    vertical_hit = jnp.any(vertical_rows[:, :, None] == key_blocks[None, None, :], axis=1)
    distance = query_blocks[:, None] - key_blocks[None, :]
    slash_hit = jnp.zeros((slash_rows.shape[0],) + distance.shape, jnp.bool_)
    for column in range(slash_rows.shape[1]):
        slash_hit = slash_hit | (slash_rows[:, column][:, None, None] == distance[None])
    causal = key_pos[None, :] <= query_pos[:, None]
    return causal[None] & (vertical_hit[:, None, :] | slash_hit)


def attend(carried, query_group, key_group, value_group, allowed, score_scale):
    max_old, totals_old, sums_old = carried
    scores = (
        jnp.einsum("qgh,kgh->gqk", query_group, key_group, preferred_element_type=jnp.float32)
        * score_scale
    )
    masked = jnp.where(allowed, scores, floor_value)
    max_new = jnp.maximum(max_old, jnp.max(masked, axis=2))
    weights = jnp.exp(masked - max_new[:, :, None])
    totals_new = jnp.sum(weights, axis=2)
    mixture = jnp.einsum(
        "gqk,kgh->qgh",
        weights.astype(jnp.bfloat16),
        value_group,
        preferred_element_type=jnp.float32,
    )
    return (max_new, totals_new, mixture)


def per_device(queries, keys, values, vertical, slash, plan):
    slot_count = plan.shape[0] // lax.axis_size("head")
    query_len = queries.shape[0]
    key_len = keys.shape[0]
    group_size = QH // KVH
    my_heads = lax.dynamic_slice_in_dim(plan, lax.axis_index("head") * slot_count, slot_count)
    kv_index = my_heads // group_size
    slot_column = jnp.arange(slot_count, dtype=jnp.int32)
    key_pick = jnp.take(keys.reshape(key_len, KVH, HD), kv_index, axis=1).reshape(
        key_len, slot_count * HD
    )
    value_pick = jnp.take(values.reshape(key_len, KVH, HD), kv_index, axis=1).reshape(
        key_len, slot_count * HD
    )
    gathered = lax.all_gather(queries, "head", axis=1, tiled=True)
    query_sel = jnp.take(gathered.reshape(query_len, QH, HD), my_heads, axis=1)
    vertical_sel = jnp.take(vertical, my_heads, axis=0)
    slash_sel = jnp.take(slash, my_heads, axis=0)
    query_pos = lax.axis_index("seq") * query_len + jnp.arange(query_len, dtype=jnp.int32)
    query_blocks = query_pos // BLK
    score_scale = HD ** (-0.5)

    def select_rows(rows):
        return jnp.take(rows.reshape(rows.shape[0], slot_count, HD), slot_column, axis=1)

    initial = (
        jnp.full((slot_count, query_len), floor_value, jnp.float32),
        jnp.zeros((slot_count, query_len), jnp.float32),
        jnp.zeros((query_len, slot_count, HD), jnp.float32),
    )
    key_piece = select_rows(lax.all_gather(key_pick, "seq", axis=0, tiled=True))
    value_piece = select_rows(lax.all_gather(value_pick, "seq", axis=0, tiled=True))
    piece_len = key_piece.shape[0]
    key_pos = jnp.arange(piece_len, dtype=jnp.int32)
    allowed = block_mask(query_blocks, key_pos // BLK, vertical_sel, slash_sel, query_pos, key_pos)
    max_parts = []
    total_parts = []
    sum_parts = []
    for lead in range(0, slot_count, 2):
        previous = (
            initial[0][lead : lead + 2],
            initial[1][lead : lead + 2],
            initial[2][:, lead : lead + 2],
        )
        updated = attend(
            previous,
            query_sel[:, lead : lead + 2],
            key_piece[:, lead : lead + 2],
            value_piece[:, lead : lead + 2],
            allowed[lead : lead + 2],
            score_scale,
        )
        max_parts.append(updated[0])
        total_parts.append(updated[1])
        sum_parts.append(updated[2])
    output = (
        jnp.concatenate(sum_parts, axis=1)
        / jnp.transpose(jnp.concatenate(total_parts, axis=0))[:, :, None]
    )
    return output.reshape(query_len, slot_count * HD).astype(jnp.bfloat16)


def solution(mesh):
    in_specs = (P("seq", "head"), P("seq", None), P("seq", None), P(), P(), P())
    out_specs = P("seq", "head")
    return jax.shard_map(
        per_device, mesh=mesh, in_specs=in_specs, out_specs=out_specs, check_vma=False
    )
```

profile of v0, /device:TPU:0, one launch (start us, length us, event | category | flops | bytes accessed | tf_op | source)
XLA Modules:
  0.0 129.1 jit_solution(5118016843818644944)
XLA Ops:
  6.5 0.0 copy-start
  6.5 0.0 all-gather.6.cloned.1.call-start
  6.5 0.7 all-gather.6.cloned.1.call-update
  7.3 0.0 all-gather.8.cloned.1.call-start
  7.3 0.7 compare_and_fusion
  8.1 0.0 copy-start.1
  8.1 0.0 copy-start.2
  8.1 0.6 gather_fusion.5
  8.8 0.9 copy_bitcast_fusion.4
  9.7 0.6 gather_fusion.1
  10.3 0.1 select_bitcast_fusion.2
  10.4 0.8 copy.49
  11.2 0.0 all-gather.8.cloned.1.call-update
  11.2 0.0 all-gather.4.cloned.1.call-start
  11.2 0.8 copy.48
  12.0 0.0 all-gather.4.cloned.1.call-update
  12.0 0.0 copy-done.1
  12.0 0.1 copy.28
  12.1 0.1 copy.29
  12.2 0.6 gather_fusion.3
  12.8 0.6 gather_fusion.4
  13.4 0.1 broadcast_select_fusion.2
  13.5 0.3 slice_reduce_fusion.7
  13.8 0.2 compare_reduce_fusion
  13.9 0.1 iota_compare_fusion
  14.0 0.1 broadcast_subtract_fusion
  14.1 2.1 %or_and_fusion = pred[16,64,512]{2,1,0:T(32,128)(4,1)S(1)} fusion(s32[64,512]{1,0:T(8,128)S(1)} %broadcast_subtract_fusion, s32[16]{0:T(128)S(1)} %get-tuple-element.8, s32[16]{0:T(128)S(1)} %get-tuple-element.10, s32[16]{0:T(128)S(1)} %get-tuple-element.11, s32[16]{0:T(128)S(1)} %get-tuple-element.12, s32[16]{0:T(128)S(1)} %get-tuple-element.13, ...), kind=kLoop, calls=%fused_computation.9 | loop fusion | flops 8912896 | bytes 696832 | tf_op jit(solution)/shard_map/and | solution.py:22
  16.2 23.4 %all-gather.6.cloned.1.call-done = bf16[64,8192]{1,0:T(8,128)(2,1)} async-done(((bf16[64,2048]{1,0:T(8,128)(2,1)}), bf16[64,8192]{1,0:T(8,128)(2,1)}) %all-gather.6.cloned.1.call-update) | async-done | bytes 1048592 | tf_op jit(solution)/shard_map/all_gather | solution.py:58
  39.6 1.5 %copy_bitcast_fusion = bf16[64,64,128]{2,0,1:T(8,128)(2,1)S(1)} fusion(bf16[64,8192]{1,0:T(8,128)(2,1)} %all-gather.6.cloned.1.call-done), kind=kLoop, calls=%fused_computation.42 | loop fusion | bytes 2097152 | tf_op jit(solution)/shard_map/reshape | solution.py:59
  41.1 0.6 gather_fusion
  41.7 27.2 %all-gather.8.cloned.1.call-done = bf16[512,2048]{1,0:T(8,128)(2,1)} async-done(((bf16[64,2048]{1,0:T(8,128)(2,1)}), bf16[512,2048]{1,0:T(8,128)(2,1)}) %all-gather.8.cloned.1.call-update) | async-done | bytes 2097168 | tf_op jit(solution)/shard_map/all_gather | solution.py:74
  68.9 3.9 %copy.33 = bf16[512,2048]{0,1:T(8,128)(2,1)} copy(bf16[512,2048]{1,0:T(8,128)(2,1)} %all-gather.8.cloned.1.call-done) | data formatting | bytes 4194304 | tf_op jit(solution)/shard_map/all_gather | solution.py:74
  72.8 3.0 %copy.34 = bf16[512,16,128]{2,0,1:T(8,128)(2,1)S(1)} copy(bf16[512,16,128]{0,2,1:T(8,128)(2,1)} %bitcast.104) | data formatting | bytes 4194304 | tf_op jit(solution)/shard_map/reshape | solution.py:67
  75.9 22.9 %all-gather.4.cloned.1.call-done = bf16[512,2048]{1,0:T(8,128)(2,1)} async-done(((bf16[64,2048]{1,0:T(8,128)(2,1)}), bf16[512,2048]{1,0:T(8,128)(2,1)}) %all-gather.4.cloned.1.call-update) | async-done | bytes 2097168 | tf_op jit(solution)/shard_map/all_gather | solution.py:75
  98.7 3.9 %copy.26 = bf16[512,2048]{0,1:T(8,128)(2,1)} copy(bf16[512,2048]{1,0:T(8,128)(2,1)} %all-gather.4.cloned.1.call-done) | data formatting | bytes 4194304 | tf_op jit(solution)/shard_map/all_gather | solution.py:75
  102.7 3.9 %copy.27 = bf16[512,16,128]{2,0,1:T(8,128)(2,1)} copy(bf16[512,16,128]{0,2,1:T(8,128)(2,1)} %bitcast.105) | data formatting | bytes 4194304 | tf_op jit(solution)/shard_map/reshape | solution.py:67
  106.6 2.1 %gather_fusion.6 = bf16[16,512,128]{2,1,0:T(8,128)(2,1)} fusion(bf16[512,16,128]{2,0,1:T(8,128)(2,1)S(1)} %copy.34, s32[1024]{0:T(1024)S(1)} %get-tuple-element.44), kind=kCustom, calls=%fused_computation.4.clone | custom fusion | bytes 4194368 | tf_op jit(solution)/shard_map/jit(_take)/gather | solution.py:67
  108.7 3.7 %gather_fusion.2 = bf16[16,512,128]{2,1,0:T(8,128)(2,1)} fusion(bf16[512,16,128]{2,0,1:T(8,128)(2,1)} %copy.27, s32[1024]{0:T(1024)S(1)} %get-tuple-element.44), kind=kCustom, calls=%fused_computation.1.clone | custom fusion | bytes 4194368 | tf_op jit(solution)/shard_map/jit(_take)/gather | solution.py:67
  112.4 2.7 %select_bitcast_fusion = (bf16[512,16,128]{2,0,1:T(8,128)(2,1)S(1)}, bf16[512,16,128]{2,0,1:T(8,128)(2,1)S(1)}) fusion(bf16[16,512,128]{2,1,0:T(8,128)(2,1)} %gather_fusion.6, pred[16]{0:T(512)(128)(4,1)S(1)} %iota_compare_fusion.1, bf16[16,512,128]{2,1,0:T(8,128)(2,1)} %gather_fusion.2), kind=kLoop, calls=%fused_computation.7 | loop fusion | flops 2097152 | bytes 8388624 | tf_op jit(solution)/shard_map/jit(_take)/select_n | solution.py:67
  115.1 0.3 fusion.83
  115.4 0.4 fusion.82
  115.8 0.4 fusion.81
  116.2 0.4 fusion.80
  116.5 0.4 fusion.79
  116.9 0.4 fusion.78
  117.2 0.4 fusion.77
  117.6 0.4 fusion.76
  118.0 0.2 fusion.41
  118.2 0.2 fusion.15
  118.5 0.2 fusion.43
  118.7 0.2 fusion.14
  118.9 0.2 fusion.45
  119.1 0.2 fusion.13
  119.4 0.2 fusion.47
  119.6 0.2 fusion.12
  119.8 0.2 fusion.49
  120.0 0.2 fusion.11
  120.2 0.2 fusion.51
  120.4 0.2 fusion.10
  120.7 0.2 fusion.53
  120.9 0.2 fusion.9
  121.1 0.2 fusion.55
  121.3 0.2 fusion.8
  121.6 0.9 copy_bitcast_fusion.1
  (18 shorter events, 0.1 us)
Async XLA Ops:
  6.5 1.5 %copy-start = (bf16[64,1024]{1,0:T(8,128)(2,1)S(1)}, bf16[64,1024]{1,0:T(8,128)(2,1)}, u32[]{:S(2)}) copy-start(bf16[64,1024]{1,0:T(8,128)(2,1)} %param.13) | copy-start | bytes 393220
  6.5 33.1 %all-gather.6.cloned.1.call-start = ((), (), s32[]{:S(2)}) async-start(), calls=%async_computation.1 | async-start | bytes 1310720 | tf_op jit(solution)/shard_map/all_gather | solution.py:58
  7.3 61.6 %all-gather.8.cloned.1.call-start = ((), (), s32[]{:S(2)}) async-start(), calls=%async_computation.2 | async-start | bytes 2359296 | tf_op jit(solution)/shard_map/all_gather | solution.py:74
  8.1 3.9 %copy-start.1 = (s32[64,8]{0,1:T(8,128)S(1)}, s32[64,8]{0,1:T(8,128)}, u32[]{:S(2)}) copy-start(s32[64,8]{0,1:T(8,128)} %param.15) | copy-start | bytes 6148
  8.1 4.0 %copy-start.2 = (s32[64,8]{0,1:T(8,128)S(1)}, s32[64,8]{0,1:T(8,128)}, u32[]{:S(2)}) copy-start(s32[64,8]{0,1:T(8,128)} %param.16) | copy-start | bytes 6148
  11.2 87.5 %all-gather.4.cloned.1.call-start = ((), (), s32[]{:S(2)}) async-start(), calls=%async_computation | async-start | bytes 2359296 | tf_op jit(solution)/shard_map/all_gather | solution.py:75
Sparse Core Ops, SparseCore 0:
  8.9 30.6 all-gather.5
  41.5 27.3 all-gather.7
  70.8 27.8 all-gather.3
where the time goes:
time: 130 us; the launch traced here: 129 us
  waiting for transfers between devices  74.1 us (57%)
  local copies, waits for them, and re-layouts  28.1 us (22%)
  between operations  13.4 us (10%)
  other arithmetic  8.55 us (7%)
  matrix products  4.79 us (4%)
    all_gather x1, waiting for transfers between devices, per_device(): key_piece = select_rows(lax.all_gather(key_pick, 'seq', axis=0, tiled=True))  27.2 us
    all_gather x1, waiting for transfers between devices, per_device(): gathered = lax.all_gather(queries, 'head', axis=1, tiled=True)  23.4 us
    all_gather x1, waiting for transfers between devices, per_device(): lax.all_gather(value_pick, 'seq', axis=0, tiled=True)  22.9 us
    reshape x2, local copies, waits for them, and re-layouts, select_rows(): rows.reshape(rows.shape[0], slot_count, HD)  6.95 us
    gather x2, local copies, waits for them, and re-layouts, select_rows(): jnp.take(rows.reshape(rows.shape[0], slot_count, HD), slot_column, axis=1)  5.84 us
    all_gather x1, local copies, waits for them, and re-layouts, per_device(): lax.all_gather(value_pick, 'seq', axis=0, tiled=True)  3.93 us
    all_gather x1, local copies, waits for them, and re-layouts, per_device(): key_piece = select_rows(lax.all_gather(key_pick, 'seq', axis=0, tiled=True))  3.93 us
    dot_general x8, matrix products, attend(): jnp.einsum('qgh,kgh->gqk', query_group, key_group, preferred_element_type...  2.82 us
  transfers between devices with their start and end apart: 3, of which 3 were waited for; matrix products, arithmetic and copies ran while one was open for 14% of the time, Pallas kernels for 0%

commit v1 on v0

v1 whole, which is shorter than its diff:
```python
import functools

import jax
import jax.numpy as jnp
from jax import lax
from jax.experimental import pallas as pl
from jax.experimental.pallas import tpu as pltpu
from jax.sharding import PartitionSpec as P

HD = 128
QH = 64
KVH = 8
BLK = 64
GROUP = QH // KVH

floor_value = -1e30


def entry_bits(table, row):
    bits = jnp.int32(0)
    for entry in range(table.shape[1]):
        named = table[row, entry]
        bits = bits | jnp.where(named >= 0, jnp.int32(1) << jnp.maximum(named, 0), 0)
    return bits


def attention_kernel(seq_size, head_size, slot_count, plan, vertical, slash, *refs):
    query_refs = refs[:head_size]
    kv_refs = refs[head_size : head_size + seq_size]
    out_ref = refs[-1]
    query_len = out_ref.shape[0]
    key_len = kv_refs[0].shape[0]
    held_heads = query_refs[0].shape[1] // HD
    own_seq = lax.axis_index("seq")
    own_head = lax.axis_index("head")

    back = lax.broadcasted_iota(jnp.int32, (1, seq_size * key_len), 1) // key_len
    block = own_seq - back
    block_shift = jnp.maximum(block, 0)
    row = lax.broadcasted_iota(jnp.int32, (query_len, seq_size * key_len), 0)
    column = lax.broadcasted_iota(jnp.int32, (query_len, seq_size * key_len), 1)
    causal = (column <= row) | (column >= key_len)
    score_scale = HD ** (-0.5)

    def slot(j):
        head = plan[own_head * slot_count + j]
        owner = head // held_heads
        held_at = pl.multiple_of((head - owner * held_heads) * HD, HD)
        steps = own_head - owner
        steps = jnp.where(steps < 0, steps + head_size, steps)
        query = query_refs[0][:, pl.ds(held_at, HD)]
        for d in range(1, head_size):
            query = jnp.where(steps == d, query_refs[d][:, pl.ds(held_at, HD)], query)
        kv_head = head // GROUP
        key_at = pl.multiple_of(kv_head * HD, HD)
        value_at = pl.multiple_of((kv_head + KVH) * HD, HD)
        key = jnp.concatenate([ref[:, pl.ds(key_at, HD)] for ref in kv_refs], axis=0)
        value = jnp.concatenate([ref[:, pl.ds(value_at, HD)] for ref in kv_refs], axis=0)
        vertical_bits = entry_bits(vertical, head)
        slash_bits = entry_bits(slash, head)
        hit = ((vertical_bits >> block_shift) | (slash_bits >> back)) & 1
        listed = (hit == 1) & (block >= 0)
        scores = lax.dot_general(
            query, key, (((1,), (1,)), ((), ())), preferred_element_type=jnp.float32
        )
        masked = jnp.where(causal & listed, scores, floor_value)
        row_max = jnp.max(masked, axis=1, keepdims=True)
        weights = jnp.exp((masked - row_max) * score_scale)
        totals = jnp.sum(weights, axis=1, keepdims=True)
        mixture = jnp.dot(
            weights.astype(jnp.bfloat16), value, preferred_element_type=jnp.float32
        )
        out_ref[:, pl.ds(pl.multiple_of(j * HD, HD), HD)] = (mixture / totals).astype(out_ref.dtype)

    for j in range(slot_count):
        slot(j)


def per_device(queries, keys, values, vertical, slash, plan):
    seq_size = lax.axis_size("seq")
    head_size = lax.axis_size("head")
    slot_count = plan.shape[0] // head_size
    query_len = queries.shape[0]
    assert query_len == BLK

    kv = jnp.concatenate([keys, values], axis=1)
    query_pieces = [queries]
    for d in range(1, head_size):
        query_pieces.append(
            lax.ppermute(queries, "head", [(i, (i + d) % head_size) for i in range(head_size)])
        )
    kv_pieces = [kv]
    for d in range(1, seq_size):
        kv_pieces.append(lax.ppermute(kv, "seq", [(i, i + d) for i in range(seq_size - d)]))

    smem = pl.BlockSpec(memory_space=pltpu.SMEM)
    vmem = pl.BlockSpec(memory_space=pltpu.VMEM)
    return pl.pallas_call(
        functools.partial(attention_kernel, seq_size, head_size, slot_count),
        out_shape=jax.ShapeDtypeStruct((query_len, slot_count * HD), jnp.bfloat16),
        in_specs=[smem] * 3 + [vmem] * (head_size + seq_size),
        out_specs=vmem,
        compiler_params=pltpu.CompilerParams(vmem_limit_bytes=40 * 1024 * 1024),
        name="attention",
    )(plan, vertical, slash, *query_pieces, *kv_pieces)


def solution(mesh):
    in_specs = (P("seq", "head"), P("seq", None), P("seq", None), P(), P(), P())
    out_specs = P("seq", "head")
    return jax.shard_map(
        per_device, mesh=mesh, in_specs=in_specs, out_specs=out_specs, check_vma=False
    )
```

time: 130 us -> 53.4 us (0.41)
  waiting for transfers between devices: 74.1 us -> 24.6 us
  local copies, waits for them, and re-layouts: 28.1 us -> 1.17 us
  starting transfers between devices: 0.08 us -> 20.6 us
  between operations: 13.4 us -> 0.12 us
  other arithmetic: 8.55 us -> 0 us
  Pallas kernels: 0 us -> 6.55 us
  matrix products: 4.79 us -> 0 us
    all_gather x3 -> x0, waiting for transfers between devices: 73.4 us -> none  [the longest x1 27.2 us: per_device(): key_piece = select_rows(lax.all_gather(key_pick, 'seq', axis=0, tiled=True))]
    ppermute x0 -> x10, waiting for transfers between devices: none -> 24.6 us  [the longest x7 13.8 us: per_device(): lax.ppermute(kv, 'seq', [(i, i + d) for i in range(seq_size - d)])]
    ppermute x0 -> x10, starting transfers between devices: none -> 20.6 us  [the longest x7 14.2 us: per_device(): lax.ppermute(kv, 'seq', [(i, i + d) for i in range(seq_size - d)])]
    reshape x7 -> x0, local copies, waits for them, and re-layouts: 10.9 us -> none  [the longest x2 6.95 us: select_rows(): rows.reshape(rows.shape[0], slot_count, HD)]
    gather x7 -> x0, local copies, waits for them, and re-layouts: 8.76 us -> none  [the longest x2 5.84 us: select_rows(): jnp.take(rows.reshape(rows.shape[0], slot_count, HD), slot_column, axis=1)]
    all_gather x2 -> x0, local copies, waits for them, and re-layouts: 7.87 us -> none  [the longest x1 3.93 us: per_device(): lax.all_gather(value_pick, 'seq', axis=0, tiled=True)]
    pallas_call x0 -> x1, Pallas kernels: none -> 6.55 us  [per_device(): pl.pallas_call(functools.partial(attention_kernel, seq_size, head_size, s...]
    dot_general x16 -> x0, matrix products: 4.79 us -> none  [the longest x8 2.82 us: attend(): jnp.einsum('qgh,kgh->gqk', query_group, key_group, preferred_element_type...]
  transfers between devices with their start and end apart: 3 -> 10, of which waited for: 3 -> 5; matrix products, arithmetic and copies ran while one was open for 14% -> 0% of each run, Pallas kernels for 0% -> 0%
where the time goes in v1:
time: 53.4 us; the launch traced here: 53.1 us
  waiting for transfers between devices  24.6 us (46%)
  starting transfers between devices  20.6 us (39%)
  Pallas kernels  6.55 us (12%)
  local copies, waits for them, and re-layouts  1.17 us (2%)
    ppermute x7, starting transfers between devices, per_device(): lax.ppermute(kv, 'seq', [(i, i + d) for i in range(seq_size - d)])  14.2 us
    ppermute x7, waiting for transfers between devices, per_device(): lax.ppermute(kv, 'seq', [(i, i + d) for i in range(seq_size - d)])  13.8 us
    ppermute x3, waiting for transfers between devices, per_device(): lax.ppermute(queries, 'head', [(i, (i + d) % head_size) for i in range(he...  10.8 us
    pallas_call x1, Pallas kernels, per_device(): pl.pallas_call(functools.partial(attention_kernel, seq_size, head_size, s...  6.55 us
    ppermute x3, starting transfers between devices, per_device(): lax.ppermute(queries, 'head', [(i, (i + d) % head_size) for i in range(he...  6.41 us
    unnamed x13, local copies, waits for them, and re-layouts  1.16 us
  transfers between devices with their start and end apart: 10, of which 5 were waited for; matrix products, arithmetic and copies ran while one was open for 0% of the time, Pallas kernels for 0%

profile of v1, /device:TPU:0, one launch (start us, length us, event | category | flops | bytes accessed | tf_op | source)
XLA Modules:
  0.0 53.1 jit_solution(2859407705293546137)
XLA Ops:
  0.0 0.0 copy-start.2
  0.0 0.0 copy-start
  0.0 1.0 %constant_dynamic-update-slice_fusion.1 = bf16[64,2048]{1,0:T(8,128)(2,1)S(1)} fusion(bf16[64,1024]{1,0:T(8,128)(2,1)} %param.7), kind=kLoop, calls=%fused_computation.1 | loop fusion | bytes 262144
  1.0 0.0 copy-done.2
  1.0 0.0 copy-start.3
  1.0 0.0 copy-start.4
  1.0 5.3 %collective-permute-start.9 = (bf16[64,2048]{1,0:T(8,128)(2,1)S(1)}, bf16[64,2048]{1,0:T(8,128)(2,1)S(1)}, u32[]{:S(2)}, u32[]{:S(2)}) collective-permute-start(bf16[64,2048]{1,0:T(8,128)(2,1)S(1)} %constant_dynamic-update-slice_fusion.refs_4_), channel_id=1, source_target_pairs={{0,28},{1,29},{2,30},{3,31}} | collective-permute-start | bytes 786440 | tf_op jit(solution)/shard_map/ppermute | solution.py:94
  6.3 1.3 %collective-permute-start.8 = (bf16[64,2048]{1,0:T(8,128)(2,1)S(1)}, bf16[64,2048]{1,0:T(8,128)(2,1)S(1)}, u32[]{:S(2)}, u32[]{:S(2)}) collective-permute-start(bf16[64,2048]{1,0:T(8,128)(2,1)S(1)} %constant_dynamic-update-slice_fusion.refs_4_), channel_id=1, source_target_pairs={{0,24},{4,28},{1,25},{5,29},{2,26},{6,30},{3,27},{7,31}} | collective-permute-start | bytes 786440 | tf_op jit(solution)/shard_map/ppermute | solution.py:94
  7.6 1.3 %collective-permute-start.7 = (bf16[64,2048]{1,0:T(8,128)(2,1)S(1)}, bf16[64,2048]{1,0:T(8,128)(2,1)S(1)}, u32[]{:S(2)}, u32[]{:S(2)}) collective-permute-start(bf16[64,2048]{1,0:T(8,128)(2,1)S(1)} %constant_dynamic-update-slice_fusion.refs_4_), channel_id=1, source_target_pairs={{0,20},{4,24},{8,28},{1,21},{5,25},{9,29},{2,22},{6,26},{10,30},{3... | collective-permute-start | bytes 786440 | tf_op jit(solution)/shard_map/ppermute | solution.py:94
  8.9 1.3 %collective-permute-start.6 = (bf16[64,2048]{1,0:T(8,128)(2,1)S(1)}, bf16[64,2048]{1,0:T(8,128)(2,1)S(1)}, u32[]{:S(2)}, u32[]{:S(2)}) collective-permute-start(bf16[64,2048]{1,0:T(8,128)(2,1)S(1)} %constant_dynamic-update-slice_fusion.refs_4_), channel_id=1, source_target_pairs={{0,16},{4,20},{8,24},{12,28},{1,17},{5,21},{9,25},{13,29},{2,18},{... | collective-permute-start | bytes 786440 | tf_op jit(solution)/shard_map/ppermute | solution.py:94
  10.2 2.2 %collective-permute-start.5 = (bf16[64,2048]{1,0:T(8,128)(2,1)S(1)}, bf16[64,2048]{1,0:T(8,128)(2,1)S(1)}, u32[]{:S(2)}, u32[]{:S(2)}) collective-permute-start(bf16[64,2048]{1,0:T(8,128)(2,1)S(1)} %constant_dynamic-update-slice_fusion.refs_4_), channel_id=1, source_target_pairs={{0,12},{4,16},{8,20},{12,24},{16,28},{1,13},{5,17},{9,21},{13,25},... | collective-permute-start | bytes 786440 | tf_op jit(solution)/shard_map/ppermute | solution.py:94
  12.4 0.0 collective-permute-done.9.refs_11_
  12.4 1.6 %collective-permute-start.4 = (bf16[64,2048]{1,0:T(8,128)(2,1)S(1)}, bf16[64,2048]{1,0:T(8,128)(2,1)S(1)}, u32[]{:S(2)}, u32[]{:S(2)}) collective-permute-start(bf16[64,2048]{1,0:T(8,128)(2,1)S(1)} %constant_dynamic-update-slice_fusion.refs_4_), channel_id=1, source_target_pairs={{0,8},{4,12},{8,16},{12,20},{16,24},{20,28},{1,9},{5,13},{9,17},{1... | collective-permute-start | bytes 786440 | tf_op jit(solution)/shard_map/ppermute | solution.py:94
  14.0 3.9 %collective-permute-done.8.refs_10_ = bf16[64,2048]{1,0:T(8,128)(2,1)S(1)} collective-permute-done((bf16[64,2048]{1,0:T(8,128)(2,1)S(1)}, bf16[64,2048]{1,0:T(8,128)(2,1)S(1)}, u32[]{:S(2)}, u32[]{:S(2)}) %collective-permute-start.8) | collective-permute-done | bytes 262176 | tf_op jit(solution)/shard_map/ppermute | solution.py:94
  17.9 1.3 %collective-permute-start.3 = (bf16[64,2048]{1,0:T(8,128)(2,1)S(1)}, bf16[64,2048]{1,0:T(8,128)(2,1)S(1)}, u32[]{:S(2)}, u32[]{:S(2)}) collective-permute-start(bf16[64,2048]{1,0:T(8,128)(2,1)S(1)} %constant_dynamic-update-slice_fusion.refs_4_), channel_id=1, source_target_pairs={{0,4},{4,8},{8,12},{12,16},{16,20},{20,24},{24,28},{1,5},{5,9},{9,... | collective-permute-start | bytes 786440 | tf_op jit(solution)/shard_map/ppermute | solution.py:94
  19.2 6.9 %collective-permute-done.7.refs_9_ = bf16[64,2048]{1,0:T(8,128)(2,1)S(1)} collective-permute-done((bf16[64,2048]{1,0:T(8,128)(2,1)S(1)}, bf16[64,2048]{1,0:T(8,128)(2,1)S(1)}, u32[]{:S(2)}, u32[]{:S(2)}) %collective-permute-start.7) | collective-permute-done | bytes 262176 | tf_op jit(solution)/shard_map/ppermute | solution.py:94
  26.1 0.0 copy-done
  26.1 2.6 %collective-permute-start.1 = (bf16[64,2048]{1,0:T(8,128)(2,1)S(1)}, bf16[64,2048]{1,0:T(8,128)(2,1)S(1)}, u32[]{:S(2)}, u32[]{:S(2)}) collective-permute-start(bf16[64,2048]{1,0:T(8,128)(2,1)S(1)} %copy-done), channel_id=1, source_target_pairs={{0,2},{1,3},{2,0},{3,1},{4,6},{5,7},{6,4},{7,5},{8,10},{9,11},{10,... | collective-permute-start | bytes 786440 | tf_op jit(solution)/shard_map/ppermute | solution.py:90
  28.7 3.0 %collective-permute-done.6.refs_8_ = bf16[64,2048]{1,0:T(8,128)(2,1)S(1)} collective-permute-done((bf16[64,2048]{1,0:T(8,128)(2,1)S(1)}, bf16[64,2048]{1,0:T(8,128)(2,1)S(1)}, u32[]{:S(2)}, u32[]{:S(2)}) %collective-permute-start.6) | collective-permute-done | bytes 262176 | tf_op jit(solution)/shard_map/ppermute | solution.py:94
  31.7 1.6 %collective-permute-start = (bf16[64,2048]{1,0:T(8,128)(2,1)S(1)}, bf16[64,2048]{1,0:T(8,128)(2,1)S(1)}, u32[]{:S(2)}, u32[]{:S(2)}) collective-permute-start(bf16[64,2048]{1,0:T(8,128)(2,1)S(1)} %copy-done), channel_id=1, source_target_pairs={{0,1},{1,2},{2,3},{3,0},{4,5},{5,6},{6,7},{7,4},{8,9},{9,10},{10,1... | collective-permute-start | bytes 786440 | tf_op jit(solution)/shard_map/ppermute | solution.py:90
  33.3 0.0 collective-permute-done.5.refs_7_
  33.3 2.2 %collective-permute-start.2 = (bf16[64,2048]{1,0:T(8,128)(2,1)S(1)}, bf16[64,2048]{1,0:T(8,128)(2,1)S(1)}, u32[]{:S(2)}, u32[]{:S(2)}) collective-permute-start(bf16[64,2048]{1,0:T(8,128)(2,1)S(1)} %copy-done), channel_id=1, source_target_pairs={{0,3},{1,0},{2,1},{3,2},{4,7},{5,4},{6,5},{7,6},{8,11},{9,8},{10,9... | collective-permute-start | bytes 786440 | tf_op jit(solution)/shard_map/ppermute | solution.py:90
  35.6 0.0 copy-done.3
  35.6 0.1 copy.7.vertical
  35.7 0.0 copy-done.4
  35.7 0.0 copy-start.1
  35.7 0.1 copy.8.slash
  35.8 0.0 collective-permute-done.4.refs_6_
  35.8 0.0 collective-permute-done.3.refs_5_
  35.8 7.7 %collective-permute-done.1.refs_2_ = bf16[64,2048]{1,0:T(8,128)(2,1)S(1)} collective-permute-done((bf16[64,2048]{1,0:T(8,128)(2,1)S(1)}, bf16[64,2048]{1,0:T(8,128)(2,1)S(1)}, u32[]{:S(2)}, u32[]{:S(2)}) %collective-permute-start.1) | collective-permute-done | bytes 262176 | tf_op jit(solution)/shard_map/ppermute | solution.py:90
  43.5 0.0 collective-permute-done.refs_1_
  43.5 3.1 %collective-permute-done.2.refs_3_ = bf16[64,2048]{1,0:T(8,128)(2,1)S(1)} collective-permute-done((bf16[64,2048]{1,0:T(8,128)(2,1)S(1)}, bf16[64,2048]{1,0:T(8,128)(2,1)S(1)}, u32[]{:S(2)}, u32[]{:S(2)}) %collective-permute-start.2) | collective-permute-done | bytes 262176 | tf_op jit(solution)/shard_map/ppermute | solution.py:90
  46.5 0.0 copy-done.1
  46.6 6.5 %attention.1 = bf16[64,2048]{1,0:T(8,128)(2,1)} custom-call(s32[64]{0:T(128)S(1)} %copy-done.1, s32[64,8]{1,0:T(8,128)S(1)} %copy.7.vertical, s32[64,8]{1,0:T(8,128)S(1)} %copy.8.slash, bf16[64,2048]{1,0:T(8,128)(2,1)S(1)} %copy-done, bf16[64,2048]{1,0:T(8,128)(2,1)S(1)} %collective-permute-done.refs_1_, ...), custom_call_target="tpu_custom_call" | custom-call | tf_op jit(solution)/shard_map/attention/pallas_call | solution.py:98
  (1 shorter events, 0.0 us)
Async XLA Ops:
  0.0 1.0 %copy-start.2 = (bf16[64,1024]{1,0:T(8,128)(2,1)S(1)}, bf16[64,1024]{1,0:T(8,128)(2,1)}, u32[]{:S(2)}) copy-start(bf16[64,1024]{1,0:T(8,128)(2,1)} %param.8) | copy-start | bytes 393220
  0.0 26.1 %copy-start = (bf16[64,2048]{1,0:T(8,128)(2,1)S(1)}, bf16[64,2048]{1,0:T(8,128)(2,1)}, u32[]{:S(2)}) copy-start(bf16[64,2048]{1,0:T(8,128)(2,1)} %refs_0_.1) | copy-start | bytes 786436
  1.0 34.6 %copy-start.3 = (s32[64,8]{0,1:T(8,128)S(1)}, s32[64,8]{0,1:T(8,128)}, u32[]{:S(2)}) copy-start(s32[64,8]{0,1:T(8,128)} %param.9) | copy-start | bytes 6148
  1.0 34.6 %copy-start.4 = (s32[64,8]{0,1:T(8,128)S(1)}, s32[64,8]{0,1:T(8,128)}, u32[]{:S(2)}) copy-start(s32[64,8]{0,1:T(8,128)} %param.10) | copy-start | bytes 6148
  1.0 11.4 %collective-permute-start.9 = (bf16[64,2048]{1,0:T(8,128)(2,1)S(1)}, bf16[64,2048]{1,0:T(8,128)(2,1)S(1)}, u32[]{:S(2)}, u32[]{:S(2)}) collective-permute-start(bf16[64,2048]{1,0:T(8,128)(2,1)S(1)} %constant_dynamic-update-slice_fusion.refs_4_), channel_id=1, source_target_pairs={{0,28},{1,29},{2,30},{3,31}} | collective-permute-start | bytes 786440 | tf_op jit(solution)/shard_map/ppermute | solution.py:94
  6.3 11.6 %collective-permute-start.8 = (bf16[64,2048]{1,0:T(8,128)(2,1)S(1)}, bf16[64,2048]{1,0:T(8,128)(2,1)S(1)}, u32[]{:S(2)}, u32[]{:S(2)}) collective-permute-start(bf16[64,2048]{1,0:T(8,128)(2,1)S(1)} %constant_dynamic-update-slice_fusion.refs_4_), channel_id=1, source_target_pairs={{0,24},{4,28},{1,25},{5,29},{2,26},{6,30},{3,27},{7,31}} | collective-permute-start | bytes 786440 | tf_op jit(solution)/shard_map/ppermute | solution.py:94
  7.6 18.5 %collective-permute-start.7 = (bf16[64,2048]{1,0:T(8,128)(2,1)S(1)}, bf16[64,2048]{1,0:T(8,128)(2,1)S(1)}, u32[]{:S(2)}, u32[]{:S(2)}) collective-permute-start(bf16[64,2048]{1,0:T(8,128)(2,1)S(1)} %constant_dynamic-update-slice_fusion.refs_4_), channel_id=1, source_target_pairs={{0,20},{4,24},{8,28},{1,21},{5,25},{9,29},{2,22},{6,26},{10,30},{3... | collective-permute-start | bytes 786440 | tf_op jit(solution)/shard_map/ppermute | solution.py:94
  8.9 22.8 %collective-permute-start.6 = (bf16[64,2048]{1,0:T(8,128)(2,1)S(1)}, bf16[64,2048]{1,0:T(8,128)(2,1)S(1)}, u32[]{:S(2)}, u32[]{:S(2)}) collective-permute-start(bf16[64,2048]{1,0:T(8,128)(2,1)S(1)} %constant_dynamic-update-slice_fusion.refs_4_), channel_id=1, source_target_pairs={{0,16},{4,20},{8,24},{12,28},{1,17},{5,21},{9,25},{13,29},{2,18},{... | collective-permute-start | bytes 786440 | tf_op jit(solution)/shard_map/ppermute | solution.py:94
  10.2 23.1 %collective-permute-start.5 = (bf16[64,2048]{1,0:T(8,128)(2,1)S(1)}, bf16[64,2048]{1,0:T(8,128)(2,1)S(1)}, u32[]{:S(2)}, u32[]{:S(2)}) collective-permute-start(bf16[64,2048]{1,0:T(8,128)(2,1)S(1)} %constant_dynamic-update-slice_fusion.refs_4_), channel_id=1, source_target_pairs={{0,12},{4,16},{8,20},{12,24},{16,28},{1,13},{5,17},{9,21},{13,25},... | collective-permute-start | bytes 786440 | tf_op jit(solution)/shard_map/ppermute | solution.py:94
  12.4 23.3 %collective-permute-start.4 = (bf16[64,2048]{1,0:T(8,128)(2,1)S(1)}, bf16[64,2048]{1,0:T(8,128)(2,1)S(1)}, u32[]{:S(2)}, u32[]{:S(2)}) collective-permute-start(bf16[64,2048]{1,0:T(8,128)(2,1)S(1)} %constant_dynamic-update-slice_fusion.refs_4_), channel_id=1, source_target_pairs={{0,8},{4,12},{8,16},{12,20},{16,24},{20,28},{1,9},{5,13},{9,17},{1... | collective-permute-start | bytes 786440 | tf_op jit(solution)/shard_map/ppermute | solution.py:94
  17.9 17.8 %collective-permute-start.3 = (bf16[64,2048]{1,0:T(8,128)(2,1)S(1)}, bf16[64,2048]{1,0:T(8,128)(2,1)S(1)}, u32[]{:S(2)}, u32[]{:S(2)}) collective-permute-start(bf16[64,2048]{1,0:T(8,128)(2,1)S(1)} %constant_dynamic-update-slice_fusion.refs_4_), channel_id=1, source_target_pairs={{0,4},{4,8},{8,12},{12,16},{16,20},{20,24},{24,28},{1,5},{5,9},{9,... | collective-permute-start | bytes 786440 | tf_op jit(solution)/shard_map/ppermute | solution.py:94
  26.1 17.3 %collective-permute-start.1 = (bf16[64,2048]{1,0:T(8,128)(2,1)S(1)}, bf16[64,2048]{1,0:T(8,128)(2,1)S(1)}, u32[]{:S(2)}, u32[]{:S(2)}) collective-permute-start(bf16[64,2048]{1,0:T(8,128)(2,1)S(1)} %copy-done), channel_id=1, source_target_pairs={{0,2},{1,3},{2,0},{3,1},{4,6},{5,7},{6,4},{7,5},{8,10},{9,11},{10,... | collective-permute-start | bytes 786440 | tf_op jit(solution)/shard_map/ppermute | solution.py:90
  31.7 11.7 %collective-permute-start = (bf16[64,2048]{1,0:T(8,128)(2,1)S(1)}, bf16[64,2048]{1,0:T(8,128)(2,1)S(1)}, u32[]{:S(2)}, u32[]{:S(2)}) collective-permute-start(bf16[64,2048]{1,0:T(8,128)(2,1)S(1)} %copy-done), channel_id=1, source_target_pairs={{0,1},{1,2},{2,3},{3,0},{4,5},{5,6},{6,7},{7,4},{8,9},{9,10},{10,1... | collective-permute-start | bytes 786440 | tf_op jit(solution)/shard_map/ppermute | solution.py:90
  33.3 13.2 %collective-permute-start.2 = (bf16[64,2048]{1,0:T(8,128)(2,1)S(1)}, bf16[64,2048]{1,0:T(8,128)(2,1)S(1)}, u32[]{:S(2)}, u32[]{:S(2)}) collective-permute-start(bf16[64,2048]{1,0:T(8,128)(2,1)S(1)} %copy-done), channel_id=1, source_target_pairs={{0,3},{1,0},{2,1},{3,2},{4,7},{5,4},{6,5},{7,6},{8,11},{9,8},{10,9... | collective-permute-start | bytes 786440 | tf_op jit(solution)/shard_map/ppermute | solution.py:90
  35.7 10.9 %copy-start.1 = (s32[64]{0:T(128)S(1)}, s32[64]{0:T(128)}, u32[]{:S(2)}) copy-start(s32[64]{0:T(128)} %plan.1) | copy-start | bytes 772

commit v2 on v1

v2 whole, which is shorter than its diff:
```python
import functools

import jax
import jax.numpy as jnp
from jax import lax
from jax.experimental import pallas as pl
from jax.experimental.pallas import tpu as pltpu
from jax.sharding import PartitionSpec as P

HD = 128
QH = 64
KVH = 8
BLK = 64
GROUP = QH // KVH
SLOTS_AT_ONCE = 4

floor_value = -1e30


def entry_bits(table, row):
    bits = jnp.int32(0)
    for entry in range(table.shape[1]):
        named = table[row, entry]
        bits = bits | jnp.where(named >= 0, jnp.int32(1) << jnp.maximum(named, 0), 0)
    return bits


def attention_kernel(seq_size, head_size, slot_count, plan, vertical, slash, *refs):
    kv_refs = refs[:seq_size]
    query_ref = refs[seq_size]
    out_ref = refs[-1]
    query_len = out_ref.shape[0]
    key_len = kv_refs[0].shape[0]
    held_heads = query_ref.shape[2] // HD
    own_seq = lax.axis_index("seq")
    own_head = lax.axis_index("head")
    chips = seq_size // 2

    piece = lax.broadcasted_iota(jnp.int32, (1, seq_size * key_len), 1) // key_len
    first_block = jnp.where(piece < chips, own_seq, own_seq + 1 - 2 * (own_seq % 2))
    block = first_block - 2 * (piece % chips)
    back = own_seq - block
    present = (block >= 0) & (back >= 0)
    block_shift = jnp.maximum(block, 0)
    back_shift = jnp.maximum(back, 0)
    row = lax.broadcasted_iota(jnp.int32, (query_len, seq_size * key_len), 0)
    column = lax.broadcasted_iota(jnp.int32, (query_len, seq_size * key_len), 1)
    causal = (column <= row) | (column >= key_len)
    score_scale = HD ** (-0.5)

    for lead in range(0, slot_count, SLOTS_AT_ONCE):
        slots = range(lead, min(lead + SLOTS_AT_ONCE, slot_count))
        heads = [plan[own_head * slot_count + j] for j in slots]
        masked = []
        for head in heads:
            owner = head // held_heads
            held_at = pl.multiple_of((head - owner * held_heads) * HD, HD)
            query = query_ref[owner, :, pl.ds(held_at, HD)]
            key_at = pl.multiple_of(head // GROUP * HD, HD)
            key = jnp.concatenate([ref[:, pl.ds(key_at, HD)] for ref in kv_refs], axis=0)
            scores = lax.dot_general(
                query, key, (((1,), (1,)), ((), ())), preferred_element_type=jnp.float32
            )
            vertical_bits = entry_bits(vertical, head)
            slash_bits = entry_bits(slash, head)
            hit = ((vertical_bits >> block_shift) | (slash_bits >> back_shift)) & 1
            listed = (hit == 1) & present
            masked.append(jnp.where(causal & listed, scores, floor_value))
        row_max = [jnp.max(m, axis=1, keepdims=True) for m in masked]
        weights = [jnp.exp((m - top) * score_scale) for m, top in zip(masked, row_max)]
        totals = [jnp.sum(w, axis=1, keepdims=True) for w in weights]
        mixture = []
        for head, w in zip(heads, weights):
            value_at = pl.multiple_of((head // GROUP + KVH) * HD, HD)
            value = jnp.concatenate([ref[:, pl.ds(value_at, HD)] for ref in kv_refs], axis=0)
            mixture.append(
                jnp.dot(w.astype(jnp.bfloat16), value, preferred_element_type=jnp.float32)
            )
        for j, mix, total in zip(slots, mixture, totals):
            out_ref[:, j * HD : (j + 1) * HD] = (mix / total).astype(out_ref.dtype)


def per_device(queries, keys, values, vertical, slash, plan):
    seq_size = lax.axis_size("seq")
    head_size = lax.axis_size("head")
    slot_count = plan.shape[0] // head_size
    query_len = queries.shape[0]
    assert query_len == BLK and seq_size % 2 == 0

    all_queries = lax.all_to_all(
        jnp.broadcast_to(queries[None], (head_size,) + queries.shape), "head", 0, 0
    )
    kv = jnp.concatenate([keys, values], axis=1)
    same_core = [kv]
    for e in range(1, seq_size // 2):
        same_core.append(lax.ppermute(kv, "seq", [(i, i + 2 * e) for i in range(seq_size - 2 * e)]))
    other_core = [lax.ppermute(kv, "seq", [(i, i + 1) for i in range(0, seq_size, 2)])]
    for e in range(1, seq_size // 2):
        pairs = [(i, i ^ 1) for i in range(2 * e, seq_size)]
        other_core.append(lax.ppermute(same_core[e], "seq", pairs))

    smem = pl.BlockSpec(memory_space=pltpu.SMEM)
    vmem = pl.BlockSpec(memory_space=pltpu.VMEM)
    return pl.pallas_call(
        functools.partial(attention_kernel, seq_size, head_size, slot_count),
        out_shape=jax.ShapeDtypeStruct((query_len, slot_count * HD), jnp.bfloat16),
        in_specs=[smem] * 3 + [vmem] * (seq_size + 1),
        out_specs=vmem,
        compiler_params=pltpu.CompilerParams(vmem_limit_bytes=40 * 1024 * 1024),
        name="attention",
    )(plan, vertical, slash, *same_core, *other_core, all_queries)


def solution(mesh):
    in_specs = (P("seq", "head"), P("seq", None), P("seq", None), P(), P(), P())
    out_specs = P("seq", "head")
    return jax.shard_map(
        per_device, mesh=mesh, in_specs=in_specs, out_specs=out_specs, check_vma=False
    )
```

time: 53.4 us -> 39.1 us (0.73)
  waiting for transfers between devices: 24.6 us -> 13.1 us
  starting transfers between devices: 20.6 us -> 17.9 us
  Pallas kernels: 6.55 us -> 4.48 us
  local copies, waits for them, and re-layouts: 1.17 us -> 3.14 us
    ppermute x10 -> x7, waiting for transfers between devices: 24.6 us -> 5.07 us  [the longest x3 5.06 us: per_device(): lax.ppermute(kv, 'seq', [(i, i + 2 * e) for i in range(seq_size - 2 * e)])]
    ppermute x10 -> x7, starting transfers between devices: 20.6 us -> 11.5 us  [the longest x3 8.14 us: per_device(): lax.ppermute(kv, 'seq', [(i, i + 2 * e) for i in range(seq_size - 2 * e)])]
    all_to_all x0 -> x1, waiting for transfers between devices: none -> 7.98 us  [per_device(): lax.all_to_all(jnp.broadcast_to(queries[None], (head_size,) + queries.sha...]
    all_to_all x0 -> x1, starting transfers between devices: none -> 6.45 us  [per_device(): lax.all_to_all(jnp.broadcast_to(queries[None], (head_size,) + queries.sha...]
    pallas_call x1, Pallas kernels: 6.55 us -> 4.48 us  [per_device(): pl.pallas_call(functools.partial(attention_kernel, seq_size, head_size, s...]
    broadcast_in_dim x0 -> x1, local copies, waits for them, and re-layouts: none -> 2.04 us  [per_device(): jnp.broadcast_to(queries[None], (head_size,) + queries.shape)]
  transfers between devices with their start and end apart: 10 -> 8, of which waited for: 5 -> 3; matrix products, arithmetic and copies ran while one was open for 0% -> 0% of each run, Pallas kernels for 0% -> 0%
where the time goes in v2:
time: 39.1 us; the launch traced here: 38.7 us
  starting transfers between devices  17.9 us (46%)
  waiting for transfers between devices  13.1 us (34%)
  Pallas kernels  4.48 us (11%)
  local copies, waits for them, and re-layouts  3.14 us (8%)
    ppermute x3, starting transfers between devices, per_device(): lax.ppermute(kv, 'seq', [(i, i + 2 * e) for i in range(seq_size - 2 * e)])  8.14 us
    all_to_all x1, waiting for transfers between devices, per_device(): lax.all_to_all(jnp.broadcast_to(queries[None], (head_size,) + queries.sha...  7.98 us
    all_to_all x1, starting transfers between devices, per_device(): lax.all_to_all(jnp.broadcast_to(queries[None], (head_size,) + queries.sha...  6.45 us
    ppermute x3, waiting for transfers between devices, per_device(): lax.ppermute(kv, 'seq', [(i, i + 2 * e) for i in range(seq_size - 2 * e)])  5.06 us
    pallas_call x1, Pallas kernels, per_device(): pl.pallas_call(functools.partial(attention_kernel, seq_size, head_size, s...  4.48 us
    broadcast_in_dim x1, local copies, waits for them, and re-layouts, per_device(): jnp.broadcast_to(queries[None], (head_size,) + queries.shape)  2.04 us
    ppermute x3, starting transfers between devices, per_device(): other_core.append(lax.ppermute(same_core[e], 'seq', pairs))  2.01 us
    ppermute x1, starting transfers between devices, per_device(): lax.ppermute(kv, 'seq', [(i, i + 1) for i in range(0, seq_size, 2)])  1.31 us
  transfers between devices with their start and end apart: 8, of which 3 were waited for; matrix products, arithmetic and copies ran while one was open for 0% of the time, Pallas kernels for 0%

profile of v2, /device:TPU:0, one launch (start us, length us, event | category | flops | bytes accessed | tf_op | source)
XLA Modules:
  0.0 38.7 jit_solution(1289310960884391050)
XLA Ops:
  0.0 2.0 %broadcast_in_dim.2 = bf16[4,64,2048]{2,1,0:T(8,128)(2,1)} broadcast(bf16[64,2048]{1,0:T(8,128)(2,1)} %param.6), dimensions={1,2} | broadcast | bytes 1310720 | tf_op jit(solution)/shard_map/broadcast_in_dim | solution.py:91
  2.0 0.0 copy-start.1
  2.0 6.4 %all-to-all-start = ((bf16[4,64,2048]{2,1,0:T(8,128)(2,1)}), bf16[4,64,2048]{2,1,0:T(8,128)(2,1)S(1)}, u32[]{:S(2)}, u32[]{:S(2)}) async-start(bf16[4,64,2048]{2,1,0:T(8,128)(2,1)} %broadcast_in_dim.2), calls=%async_computation | async-start | bytes 2097152 | tf_op jit(solution)/shard_map/all_to_all | solution.py:90
  8.5 0.0 copy-done.1
  8.5 0.0 copy-start.2
  8.5 0.9 %copy-done.2 = bf16[64,1024]{1,0:T(8,128)(2,1)S(1)} copy-done((bf16[64,1024]{1,0:T(8,128)(2,1)S(1)}, bf16[64,1024]{1,0:T(8,128)(2,1)}, u32[]{:S(2)}) %copy-start.2) | copy-done | bytes 131096
  9.4 0.0 copy-start.3
  9.4 0.0 copy-start.4
  9.4 3.4 %collective-permute-start = (bf16[64,2048]{1,0:T(8,128)(2,1)S(1)}, bf16[64,2048]{1,0:T(8,128)(2,1)S(1)}, u32[]{:S(2)}, u32[]{:S(2)}) collective-permute-start(bf16[64,2048]{1,0:T(8,128)(2,1)S(1)} %constant_dynamic-update-slice_fusion.refs_0_), channel_id=1, source_target_pairs={{0,8},{4,12},{8,16},{12,20},{16,24},{20,28},{1,9},{5,13},{9,17},{1... | collective-permute-start | bytes 786440 | tf_op jit(solution)/shard_map/ppermute | solution.py:96
  12.8 3.4 %collective-permute-start.1 = (bf16[64,2048]{1,0:T(8,128)(2,1)S(1)}, bf16[64,2048]{1,0:T(8,128)(2,1)S(1)}, u32[]{:S(2)}, u32[]{:S(2)}) collective-permute-start(bf16[64,2048]{1,0:T(8,128)(2,1)S(1)} %constant_dynamic-update-slice_fusion.refs_0_), channel_id=1, source_target_pairs={{0,16},{4,20},{8,24},{12,28},{1,17},{5,21},{9,25},{13,29},{2,18},{... | collective-permute-start | bytes 786440 | tf_op jit(solution)/shard_map/ppermute | solution.py:96
  16.3 1.3 %collective-permute-start.2 = (bf16[64,2048]{1,0:T(8,128)(2,1)S(1)}, bf16[64,2048]{1,0:T(8,128)(2,1)S(1)}, u32[]{:S(2)}, u32[]{:S(2)}) collective-permute-start(bf16[64,2048]{1,0:T(8,128)(2,1)S(1)} %constant_dynamic-update-slice_fusion.refs_0_), channel_id=1, source_target_pairs={{0,24},{4,28},{1,25},{5,29},{2,26},{6,30},{3,27},{7,31}} | collective-permute-start | bytes 786440 | tf_op jit(solution)/shard_map/ppermute | solution.py:96
  17.6 1.3 %collective-permute-start.3 = (bf16[64,2048]{1,0:T(8,128)(2,1)S(1)}, bf16[64,2048]{1,0:T(8,128)(2,1)S(1)}, u32[]{:S(2)}, u32[]{:S(2)}) collective-permute-start(bf16[64,2048]{1,0:T(8,128)(2,1)S(1)} %constant_dynamic-update-slice_fusion.refs_0_), channel_id=1, source_target_pairs={{0,4},{8,12},{16,20},{24,28},{1,5},{9,13},{17,21},{25,29},{2,6},{1... | collective-permute-start | bytes 786440 | tf_op jit(solution)/shard_map/ppermute | solution.py:97
  18.9 0.3 collective-permute-done.refs_1_
  19.2 0.7 %collective-permute-start.4 = (bf16[64,2048]{1,0:T(8,128)(2,1)S(1)}, bf16[64,2048]{1,0:T(8,128)(2,1)S(1)}, u32[]{:S(2)}, u32[]{:S(2)}) collective-permute-start(bf16[64,2048]{1,0:T(8,128)(2,1)S(1)} %collective-permute-done.refs_1_), channel_id=1, source_target_pairs={{8,12},{12,8},{16,20},{20,16},{24,28},{28,24},{9,13},{13,9},{17,21... | collective-permute-start | bytes 786440 | tf_op jit(solution)/shard_map/ppermute | solution.py:100
  19.9 4.8 %collective-permute-done.1.refs_2_ = bf16[64,2048]{1,0:T(8,128)(2,1)S(1)} collective-permute-done((bf16[64,2048]{1,0:T(8,128)(2,1)S(1)}, bf16[64,2048]{1,0:T(8,128)(2,1)S(1)}, u32[]{:S(2)}, u32[]{:S(2)}) %collective-permute-start.1) | collective-permute-done | bytes 262176 | tf_op jit(solution)/shard_map/ppermute | solution.py:96
  24.6 0.7 %collective-permute-start.5 = (bf16[64,2048]{1,0:T(8,128)(2,1)S(1)}, bf16[64,2048]{1,0:T(8,128)(2,1)S(1)}, u32[]{:S(2)}, u32[]{:S(2)}) collective-permute-start(bf16[64,2048]{1,0:T(8,128)(2,1)S(1)} %collective-permute-done.1.refs_2_), channel_id=1, source_target_pairs={{16,20},{20,16},{24,28},{28,24},{17,21},{21,17},{25,29},{29,25},{1... | collective-permute-start | bytes 786440 | tf_op jit(solution)/shard_map/ppermute | solution.py:100
  25.3 0.0 collective-permute-done.2.refs_3_
  25.3 0.7 %collective-permute-start.6 = (bf16[64,2048]{1,0:T(8,128)(2,1)S(1)}, bf16[64,2048]{1,0:T(8,128)(2,1)S(1)}, u32[]{:S(2)}, u32[]{:S(2)}) collective-permute-start(bf16[64,2048]{1,0:T(8,128)(2,1)S(1)} %collective-permute-done.2.refs_3_), channel_id=1, source_target_pairs={{24,28},{28,24},{25,29},{29,25},{26,30},{30,26},{27,31},{31,27}} | collective-permute-start | bytes 786440 | tf_op jit(solution)/shard_map/ppermute | solution.py:100
  26.0 0.0 copy-done.3
  26.0 0.1 copy.7.vertical
  26.1 0.0 copy-done.4
  26.1 0.0 copy-start
  26.1 0.1 copy.8.slash
  26.2 0.0 collective-permute-done.3.refs_4_
  26.2 0.0 collective-permute-done.4.refs_5_
  26.2 0.0 collective-permute-done.5.refs_6_
  26.2 0.0 collective-permute-done.6.refs_7_
  26.2 8.0 %all-to-all-done.refs_8_ = bf16[4,64,2048]{2,1,0:T(8,128)(2,1)S(1)} async-done(((bf16[4,64,2048]{2,1,0:T(8,128)(2,1)}), bf16[4,64,2048]{2,1,0:T(8,128)(2,1)S(1)}, u32[]{:S(2)}, u32[]{:S(2)}) %all-to-all-start) | async-done | bytes 1048608 | tf_op jit(solution)/shard_map/all_to_all | solution.py:90
  34.2 0.0 copy-done
  34.2 4.5 %attention.1 = bf16[64,2048]{1,0:T(8,128)(2,1)} custom-call(s32[64]{0:T(128)S(1)} %copy-done, s32[64,8]{1,0:T(8,128)S(1)} %copy.7.vertical, s32[64,8]{1,0:T(8,128)S(1)} %copy.8.slash, bf16[64,2048]{1,0:T(8,128)(2,1)S(1)} %constant_dynamic-update-slice_fusion.refs_0_, bf16[64,2048]{1,0:T(8,128)(2,1)S(1)} %collective-permute-done.refs_1_, ...), custom_call_target="tpu_custom_call" | custom-call | tf_op jit(solution)/shard_map/attention/pallas_call | solution.py:104
  (2 shorter events, 0.0 us)
Async XLA Ops:
  2.0 6.5 %copy-start.1 = (bf16[64,1024]{1,0:T(8,128)(2,1)S(1)}, bf16[64,1024]{1,0:T(8,128)(2,1)}, u32[]{:S(2)}) copy-start(bf16[64,1024]{1,0:T(8,128)(2,1)} %param.7) | copy-start | bytes 393220
  2.0 32.2 %all-to-all-start = ((bf16[4,64,2048]{2,1,0:T(8,128)(2,1)}), bf16[4,64,2048]{2,1,0:T(8,128)(2,1)S(1)}, u32[]{:S(2)}, u32[]{:S(2)}) async-start(bf16[4,64,2048]{2,1,0:T(8,128)(2,1)} %broadcast_in_dim.2), calls=%async_computation | async-start | bytes 2097152 | tf_op jit(solution)/shard_map/all_to_all | solution.py:90
  8.5 0.9 %copy-start.2 = (bf16[64,1024]{1,0:T(8,128)(2,1)S(1)}, bf16[64,1024]{1,0:T(8,128)(2,1)}, u32[]{:S(2)}) copy-start(bf16[64,1024]{1,0:T(8,128)(2,1)} %param.8) | copy-start | bytes 393220
  9.4 16.6 %copy-start.3 = (s32[64,8]{0,1:T(8,128)S(1)}, s32[64,8]{0,1:T(8,128)}, u32[]{:S(2)}) copy-start(s32[64,8]{0,1:T(8,128)} %param.9) | copy-start | bytes 6148
  9.4 16.7 %copy-start.4 = (s32[64,8]{0,1:T(8,128)S(1)}, s32[64,8]{0,1:T(8,128)}, u32[]{:S(2)}) copy-start(s32[64,8]{0,1:T(8,128)} %param.10) | copy-start | bytes 6148
  9.4 9.8 %collective-permute-start = (bf16[64,2048]{1,0:T(8,128)(2,1)S(1)}, bf16[64,2048]{1,0:T(8,128)(2,1)S(1)}, u32[]{:S(2)}, u32[]{:S(2)}) collective-permute-start(bf16[64,2048]{1,0:T(8,128)(2,1)S(1)} %constant_dynamic-update-slice_fusion.refs_0_), channel_id=1, source_target_pairs={{0,8},{4,12},{8,16},{12,20},{16,24},{20,28},{1,9},{5,13},{9,17},{1... | collective-permute-start | bytes 786440 | tf_op jit(solution)/shard_map/ppermute | solution.py:96
  12.8 11.8 %collective-permute-start.1 = (bf16[64,2048]{1,0:T(8,128)(2,1)S(1)}, bf16[64,2048]{1,0:T(8,128)(2,1)S(1)}, u32[]{:S(2)}, u32[]{:S(2)}) collective-permute-start(bf16[64,2048]{1,0:T(8,128)(2,1)S(1)} %constant_dynamic-update-slice_fusion.refs_0_), channel_id=1, source_target_pairs={{0,16},{4,20},{8,24},{12,28},{1,17},{5,21},{9,25},{13,29},{2,18},{... | collective-permute-start | bytes 786440 | tf_op jit(solution)/shard_map/ppermute | solution.py:96
  16.3 9.0 %collective-permute-start.2 = (bf16[64,2048]{1,0:T(8,128)(2,1)S(1)}, bf16[64,2048]{1,0:T(8,128)(2,1)S(1)}, u32[]{:S(2)}, u32[]{:S(2)}) collective-permute-start(bf16[64,2048]{1,0:T(8,128)(2,1)S(1)} %constant_dynamic-update-slice_fusion.refs_0_), channel_id=1, source_target_pairs={{0,24},{4,28},{1,25},{5,29},{2,26},{6,30},{3,27},{7,31}} | collective-permute-start | bytes 786440 | tf_op jit(solution)/shard_map/ppermute | solution.py:96
  17.6 8.6 %collective-permute-start.3 = (bf16[64,2048]{1,0:T(8,128)(2,1)S(1)}, bf16[64,2048]{1,0:T(8,128)(2,1)S(1)}, u32[]{:S(2)}, u32[]{:S(2)}) collective-permute-start(bf16[64,2048]{1,0:T(8,128)(2,1)S(1)} %constant_dynamic-update-slice_fusion.refs_0_), channel_id=1, source_target_pairs={{0,4},{8,12},{16,20},{24,28},{1,5},{9,13},{17,21},{25,29},{2,6},{1... | collective-permute-start | bytes 786440 | tf_op jit(solution)/shard_map/ppermute | solution.py:97
  19.2 7.0 %collective-permute-start.4 = (bf16[64,2048]{1,0:T(8,128)(2,1)S(1)}, bf16[64,2048]{1,0:T(8,128)(2,1)S(1)}, u32[]{:S(2)}, u32[]{:S(2)}) collective-permute-start(bf16[64,2048]{1,0:T(8,128)(2,1)S(1)} %collective-permute-done.refs_1_), channel_id=1, source_target_pairs={{8,12},{12,8},{16,20},{20,16},{24,28},{28,24},{9,13},{13,9},{17,21... | collective-permute-start | bytes 786440 | tf_op jit(solution)/shard_map/ppermute | solution.py:100
  24.6 1.6 %collective-permute-start.5 = (bf16[64,2048]{1,0:T(8,128)(2,1)S(1)}, bf16[64,2048]{1,0:T(8,128)(2,1)S(1)}, u32[]{:S(2)}, u32[]{:S(2)}) collective-permute-start(bf16[64,2048]{1,0:T(8,128)(2,1)S(1)} %collective-permute-done.1.refs_2_), channel_id=1, source_target_pairs={{16,20},{20,16},{24,28},{28,24},{17,21},{21,17},{25,29},{29,25},{1... | collective-permute-start | bytes 786440 | tf_op jit(solution)/shard_map/ppermute | solution.py:100
  25.3 0.9 %collective-permute-start.6 = (bf16[64,2048]{1,0:T(8,128)(2,1)S(1)}, bf16[64,2048]{1,0:T(8,128)(2,1)S(1)}, u32[]{:S(2)}, u32[]{:S(2)}) collective-permute-start(bf16[64,2048]{1,0:T(8,128)(2,1)S(1)} %collective-permute-done.2.refs_3_), channel_id=1, source_target_pairs={{24,28},{28,24},{25,29},{29,25},{26,30},{30,26},{27,31},{31,27}} | collective-permute-start | bytes 786440 | tf_op jit(solution)/shard_map/ppermute | solution.py:100
  26.1 8.1 %copy-start = (s32[64]{0:T(128)S(1)}, s32[64]{0:T(128)}, u32[]{:S(2)}) copy-start(s32[64]{0:T(128)} %plan.1) | copy-start | bytes 772

commit v3 on v1

v3 whole, which is shorter than its diff:
```python
import functools

import jax
import jax.numpy as jnp
from jax import lax
from jax.experimental import pallas as pl
from jax.experimental.pallas import tpu as pltpu
from jax.sharding import PartitionSpec as P

HD = 128
QH = 64
KVH = 8
BLK = 64
GROUP = QH // KVH
HEADS_AT_ONCE = 4

floor_value = -1e30

SMEM = pl.BlockSpec(memory_space=pltpu.SMEM)
VMEM = pl.BlockSpec(memory_space=pltpu.VMEM)


def shift_of(size):
    assert size & (size - 1) == 0
    return size.bit_length() - 1


def route_kernel(head_size, held, plan, send, receive, most, counts):
    own = lax.axis_index("head")
    for pair in range(head_size * head_size):
        counts[pair] = 0
    largest = jnp.int32(0)
    for slot in range(plan.shape[0]):
        target = slot // held
        head = plan[slot]
        owner = head >> shift_of(held)
        pair = owner * head_size + target
        rank = counts[pair]
        counts[pair] = rank + 1
        largest = jnp.maximum(largest, jnp.where(owner == target, 0, rank + 1))
        place = ((target - owner) & (head_size - 1)) * held + rank
        send[jnp.where(owner == own, head & (held - 1), held)] = place
        receive[jnp.where(own == target, slot % held, held)] = place
    most[0] = largest


def entry_bits(table, row):
    bits = jnp.int32(0)
    for entry in range(table.shape[1]):
        named = table[row, entry]
        bits = bits | jnp.where(named >= 0, jnp.int32(1) << jnp.maximum(named, 0), 0)
    return bits


def attention_kernel(seq_size, held, kv_heads, send, vertical, slash, kv_own, kv_other, query_ref, out_ref):
    query_len = query_ref.shape[0]
    key_len = query_len
    own_seq = lax.axis_index("seq")
    own_head = lax.axis_index("head")
    chips = seq_size // 2
    half = chips * key_len

    piece = lax.broadcasted_iota(jnp.int32, (1, 2 * half), 1) // key_len
    core = jnp.where(piece < chips, own_seq & 1, 1 - (own_seq & 1))
    block = ((own_seq >> 1) ^ (piece & (chips - 1))) * 2 + core
    back = own_seq - block
    present = back >= 0
    back_shift = jnp.maximum(back, 0)
    row = lax.broadcasted_iota(jnp.int32, (query_len, 2 * half), 0)
    column = lax.broadcasted_iota(jnp.int32, (query_len, 2 * half), 1)
    causal = (column <= row) | (column >= key_len)
    score_scale = HD ** (-0.5)
    per_kv = held // kv_heads

    for lead in range(0, held, HEADS_AT_ONCE):
        heads = range(lead, min(lead + HEADS_AT_ONCE, held))
        kv_head = lead // per_kv
        key_at = kv_head * HD
        value_at = (kv_head + kv_heads) * HD
        key = jnp.concatenate([kv_own[:, key_at : key_at + HD], kv_other[:, key_at : key_at + HD]], axis=0)
        value = jnp.concatenate(
            [kv_own[:, value_at : value_at + HD], kv_other[:, value_at : value_at + HD]], axis=0
        )
        query = jnp.concatenate([query_ref[:, i * HD : (i + 1) * HD] for i in heads], axis=0)
        scores = lax.dot_general(
            query, key, (((1,), (1,)), ((), ())), preferred_element_type=jnp.float32
        )
        weights = []
        totals = []
        for at, i in enumerate(heads):
            head = own_head * held + i
            vertical_bits = entry_bits(vertical, head)
            slash_bits = entry_bits(slash, head)
            hit = ((vertical_bits >> block) | (slash_bits >> back_shift)) & 1
            listed = (hit == 1) & present
            own_scores = scores[at * query_len : (at + 1) * query_len]
            masked = jnp.where(causal & listed, own_scores, floor_value)
            row_max = jnp.max(masked, axis=1, keepdims=True)
            weight = jnp.exp((masked - row_max) * score_scale)
            totals.append(jnp.sum(weight, axis=1, keepdims=True))
            weights.append(weight.astype(jnp.bfloat16))
        mixture = jnp.dot(
            jnp.concatenate(weights, axis=0), value, preferred_element_type=jnp.float32
        )
        for at, i in enumerate(heads):
            mix = mixture[at * query_len : (at + 1) * query_len]
            out_ref[send[i]] = (mix / totals[at]).astype(out_ref.dtype)


def place_kernel(held, receive, kept, *refs):
    arrived = refs[:-1]
    out_ref = refs[-1]
    capacity = arrived[0].shape[0]
    for t in range(out_ref.shape[1] // HD):
        place = receive[t]
        distance = place >> shift_of(held)
        rank = place & (held - 1)
        rows = kept[rank]
        rank_sent = jnp.minimum(rank, capacity - 1)
        for d, ref in enumerate(arrived):
            rows = jnp.where(distance == d + 1, ref[rank_sent], rows)
        out_ref[:, t * HD : (t + 1) * HD] = rows


def exchange(head_size, held, capacity, packed, receive):
    arrived = []
    for d in range(1, head_size):
        arrived.append(
            lax.ppermute(
                packed[d * held : d * held + capacity],
                "head",
                [(i, (i + d) % head_size) for i in range(head_size)],
            )
        )
    query_len = packed.shape[1]
    return pl.pallas_call(
        functools.partial(place_kernel, held),
        out_shape=jax.ShapeDtypeStruct((query_len, held * HD), packed.dtype),
        in_specs=[SMEM] + [VMEM] * head_size,
        out_specs=VMEM,
        name="place",
    )(receive, packed[:held], *arrived)


def per_device(queries, keys, values, vertical, slash, plan):
    seq_size = lax.axis_size("seq")
    head_size = lax.axis_size("head")
    query_len = queries.shape[0]
    held = queries.shape[1] // HD
    kv_heads = max(1, held // GROUP)
    chips = seq_size // 2
    assert query_len == BLK and plan.shape[0] == held * head_size and chips & (chips - 1) == 0

    send, receive, most = pl.pallas_call(
        functools.partial(route_kernel, head_size, held),
        out_shape=[
            jax.ShapeDtypeStruct((held + 1,), jnp.int32),
            jax.ShapeDtypeStruct((held + 1,), jnp.int32),
            jax.ShapeDtypeStruct((1,), jnp.int32),
        ],
        in_specs=[SMEM],
        out_specs=[SMEM] * 3,
        scratch_shapes=[pltpu.SMEM((head_size * head_size,), jnp.int32)],
        name="route",
    )(plan)

    kv_at = lax.axis_index("head") * held // GROUP * HD
    kv = jnp.concatenate(
        [lax.dynamic_slice_in_dim(rows, kv_at, kv_heads * HD, axis=1) for rows in (keys, values)], axis=1
    )
    pieces = [kv]
    for m in range(1, chips):
        pairs = [(i, i ^ (2 * m)) for i in range(seq_size) if i < i ^ (2 * m)]
        pieces.append(lax.ppermute(kv, "seq", pairs))
    kv_own = jnp.concatenate(pieces, axis=0)
    kv_other = lax.ppermute(kv_own, "seq", [(i, i ^ 1) for i in range(seq_size)])

    packed = pl.pallas_call(
        functools.partial(attention_kernel, seq_size, held, kv_heads),
        out_shape=jax.ShapeDtypeStruct((head_size * held, query_len, HD), jnp.bfloat16),
        in_specs=[SMEM] * 3 + [VMEM] * 3,
        out_specs=VMEM,
        compiler_params=pltpu.CompilerParams(vmem_limit_bytes=40 * 1024 * 1024),
        name="attention",
    )(send, vertical, slash, kv_own, kv_other, queries)

    capacities = sorted({c for c in (held * 3 // 8, held // 2) if c} | {held})
    level = jnp.int32(0)
    for capacity in capacities[:-1]:
        level = level + (most[0] > capacity).astype(jnp.int32)
    return lax.switch(
        level,
        [functools.partial(exchange, head_size, held, capacity) for capacity in capacities],
        packed,
        receive,
    )


def solution(mesh):
    in_specs = (P("seq", "head"), P("seq", None), P("seq", None), P(), P(), P())
    out_specs = P("seq", "head")
    return jax.shard_map(
        per_device, mesh=mesh, in_specs=in_specs, out_specs=out_specs, check_vma=False
    )
```

time: 53.4 us -> 39.1 us (0.73)
  waiting for transfers between devices: 24.6 us -> 12.3 us
  starting transfers between devices: 20.6 us -> 14.4 us
  local copies, waits for them, and re-layouts: 1.17 us -> 4.33 us
  between operations: 0.12 us -> 1.42 us
    ppermute x10 -> x7, waiting for transfers between devices: 24.6 us -> 12.3 us  [the longest x3 10.4 us: exchange(): lax.ppermute(packed[d * held:d * held + capacity], 'head', [(i, (i + d) %...]
    ppermute x10 -> x7, starting transfers between devices: 20.6 us -> 14.4 us  [the longest x3 9.7 us: per_device(): pieces.append(lax.ppermute(kv, 'seq', pairs))]
    unnamed x13 -> x12, local copies, waits for them, and re-layouts: 1.16 us -> 2.11 us
    dynamic_slice x0 -> x1, local copies, waits for them, and re-layouts: none -> 0.78 us  [per_device(): lax.dynamic_slice_in_dim(rows, kv_at, kv_heads * HD, axis=1)]
    slice x0 -> x2, local copies, waits for them, and re-layouts: none -> 0.75 us  [the longest x1 0.72 us: exchange(): packed[:held]]
    cond x0 -> x6, local copies, waits for them, and re-layouts: none -> 0.69 us
    pallas_call x1 -> x3, Pallas kernels: 6.55 us -> 6.21 us  [the longest x1 3.18 us: per_device(): pl.pallas_call(functools.partial(attention_kernel, seq_size, held, kv_hea...]
  transfers between devices with their start and end apart: 10 -> 7, of which waited for: 5 -> 3; matrix products, arithmetic and copies ran while one was open for 0% -> 2% of each run, Pallas kernels for 0% -> 5%
where the time goes in v3:
time: 39.1 us; the launch traced here: 38.7 us
  starting transfers between devices  14.4 us (37%)
  waiting for transfers between devices  12.3 us (31%)
  Pallas kernels  6.21 us (16%)
  local copies, waits for them, and re-layouts  4.33 us (11%)
  between operations  1.42 us (4%)
    ppermute x3, waiting for transfers between devices, exchange(): lax.ppermute(packed[d * held:d * held + capacity], 'head', [(i, (i + d) %...  10.4 us
    ppermute x3, starting transfers between devices, per_device(): pieces.append(lax.ppermute(kv, 'seq', pairs))  9.7 us
    ppermute x3, starting transfers between devices, exchange(): lax.ppermute(packed[d * held:d * held + capacity], 'head', [(i, (i + d) %...  4.67 us
    pallas_call x1, Pallas kernels, per_device(): pl.pallas_call(functools.partial(attention_kernel, seq_size, held, kv_hea...  3.18 us
    unnamed x12, local copies, waits for them, and re-layouts  2.11 us
    ppermute x3, waiting for transfers between devices, per_device(): pieces.append(lax.ppermute(kv, 'seq', pairs))  1.87 us
    pallas_call x1, Pallas kernels, per_device(): pl.pallas_call(functools.partial(route_kernel, head_size, held), out_shap...  1.75 us
    pallas_call x1, Pallas kernels, exchange(): pl.pallas_call(functools.partial(place_kernel, held), out_shape=jax.Shape...  1.28 us
  transfers between devices with their start and end apart: 7, of which 3 were waited for; matrix products, arithmetic and copies ran while one was open for 2% of the time, Pallas kernels for 5%

profile of v3, /device:TPU:0, one launch (start us, length us, event | category | flops | bytes accessed | tf_op | source)
XLA Modules:
  0.0 38.7 jit_solution(18400388970662085085)
XLA Ops:
  0.0 0.8 %constant_dynamic-slice_fusion = (bf16[64,256]{1,0:T(8,128)(2,1)S(1)}, bf16[64,256]{1,0:T(8,128)(2,1)S(1)}) fusion(bf16[64,1024]{1,0:T(8,128)(2,1)} %param.11, s32[]{:T(128)S(6)} %select_n.10, bf16[64,1024]{1,0:T(8,128)(2,1)} %param.10), kind=kLoop, calls=%fused_computation.2 | loop fusion | bytes 131076 | tf_op jit(solution)/shard_map/dynamic_slice | solution.py:169
  0.8 0.0 copy-start
  0.8 5.9 %collective-permute-start.11 = (bf16[64,512]{1,0:T(8,128)(2,1)S(1)}, bf16[64,512]{1,0:T(8,128)(2,1)S(1)}, u32[]{:S(2)}, u32[]{:S(2)}) collective-permute-start(bf16[64,512]{1,0:T(8,128)(2,1)S(1)} %pad_maximum_fusion.1), channel_id=1, source_target_pairs={{0,24},{4,28},{8,16},{12,20},{1,25},{5,29},{9,17},{13,21},{2,26},{... | collective-permute-start | bytes 196616 | tf_op jit(solution)/shard_map/ppermute | solution.py:174
  6.7 1.3 %collective-permute-start.10 = (bf16[64,512]{1,0:T(8,128)(2,1)S(1)}, bf16[64,512]{1,0:T(8,128)(2,1)S(1)}, u32[]{:S(2)}, u32[]{:S(2)}) collective-permute-start(bf16[64,512]{1,0:T(8,128)(2,1)S(1)} %pad_maximum_fusion.1), channel_id=1, source_target_pairs={{0,16},{4,20},{8,24},{12,28},{1,17},{5,21},{9,25},{13,29},{2,18},{... | collective-permute-start | bytes 196616 | tf_op jit(solution)/shard_map/ppermute | solution.py:174
  8.0 2.5 %collective-permute-start.9 = (bf16[64,512]{1,0:T(8,128)(2,1)S(1)}, bf16[64,512]{1,0:T(8,128)(2,1)S(1)}, u32[]{:S(2)}, u32[]{:S(2)}) collective-permute-start(bf16[64,512]{1,0:T(8,128)(2,1)S(1)} %pad_maximum_fusion.1), channel_id=1, source_target_pairs={{0,8},{4,12},{16,24},{20,28},{1,9},{5,13},{17,25},{21,29},{2,10},{... | collective-permute-start | bytes 196616 | tf_op jit(solution)/shard_map/ppermute | solution.py:174
  10.5 0.0 collective-permute-done.11
  10.5 0.0 collective-permute-done.10
  10.5 1.9 %collective-permute-done.9 = bf16[64,512]{1,0:T(8,128)(2,1)S(1)} collective-permute-done((bf16[64,512]{1,0:T(8,128)(2,1)S(1)}, bf16[64,512]{1,0:T(8,128)(2,1)S(1)}, u32[]{:S(2)}, u32[]{:S(2)}) %collective-permute-start.9) | collective-permute-done | bytes 65568 | tf_op jit(solution)/shard_map/ppermute | solution.py:174
  12.4 0.1 collective-permute-start.12
  12.5 1.7 %route.1 = (s32[17]{0:T(128)}, s32[17]{0:T(128)S(1)}, s32[1]{0:T(128)}) custom-call(s32[64]{0:T(128)} %plan.1), custom_call_target="tpu_custom_call" | custom-call | tf_op jit(solution)/shard_map/route/pallas_call | solution.py:154
  14.3 0.0 copy-start.12
  15.6 0.0 copy-done.12
  15.6 0.0 copy-start.13
  15.6 0.1 copy.10.vertical
  15.7 0.6 %copy-done.13 = s32[64,8]{0,1:T(8,128)S(1)} copy-done((s32[64,8]{0,1:T(8,128)S(1)}, s32[64,8]{0,1:T(8,128)}, u32[]{:S(2)}) %copy-start.13) | copy-done | bytes 2072
  16.3 0.1 copy.11.slash
  16.3 0.0 copy-start.1
  16.3 0.0 collective-permute-done.12.kv_other
  16.4 0.0 copy-done
  16.4 0.6 %copy-done.1 = s32[17]{0:T(128)S(1)} copy-done((s32[17]{0:T(128)S(1)}, s32[17]{0:T(128)}, u32[]{:S(2)}) %copy-start.1) | copy-done | bytes 92
  17.0 3.2 %attention.1 = bf16[64,64,128]{2,1,0:T(8,128)(2,1)S(1)} custom-call(s32[17]{0:T(128)S(1)} %copy-done.1, s32[64,8]{1,0:T(8,128)S(1)} %copy.10.vertical, s32[64,8]{1,0:T(8,128)S(1)} %copy.11.slash, bf16[256,512]{1,0:T(8,128)(2,1)S(1)} %pad_maximum_fusion.kv_own, bf16[256,512]{1,0:T(8,128)(2,1)S(1)} %collective-permute-done.12.kv_other, ...), custom_call_target="tpu_custom_call" | custom-call | tf_op jit(solution)/shard_map/attention/pallas_call | solution.py:178
  20.2 17.8 %conditional.1 = (bf16[64,2048]{1,0:T(8,128)(2,1)S(1)}) conditional(s32[]{:T(128)} %bitcast, (bf16[64,64,128]{2,1,0:T(8,128)(2,1)S(1)}, s32[17]{0:T(128)S(1)}) %tuple.14, (bf16[64,64,128]{2,1,0:T(8,128)(2,1)S(1)}, s32[17]{0:T(128)S(1)}) %tuple.14, (bf16[64,64,128]{2,1,0:T(8,128)(2,1)S(1)}, s32[17]{0:T(128)S(1)}) %tuple.14), branch_computations={%region_0.1_spmd, %region_1.2_spmd, %region_2.3_spmd} | conditional | bytes 8388820 | solution.py:191
  20.2 3.7 %collective-permute-start.5 = (bf16[8,64,128]{2,1,0:T(8,128)(2,1)S(1)}, bf16[8,64,128]{2,1,0:T(8,128)(2,1)S(1)}, u32[]{:S(2)}, u32[]{:S(2)}) collective-permute-start(bf16[8,64,128]{2,1,0:T(8,128)(2,1)S(1)} %get-tuple-element.37), channel_id=1, source_target_pairs={{0,3},{1,0},{2,1},{3,2},{4,7},{5,4},{6,5},{7,6},{8,11},{9,8},{10,9... | collective-permute-start | bytes 393224 | tf_op jit(solution)/shard_map/cond/branch_1_fun/ppermute | solution.py:129
  23.9 0.0 collective-permute-start.4
  23.9 1.0 %collective-permute-start.3 = (bf16[8,64,128]{2,1,0:T(8,128)(2,1)S(1)}, bf16[8,64,128]{2,1,0:T(8,128)(2,1)S(1)}, u32[]{:S(2)}, u32[]{:S(2)}) collective-permute-start(bf16[8,64,128]{2,1,0:T(8,128)(2,1)S(1)} %get-tuple-element.39), channel_id=1, source_target_pairs={{0,1},{1,2},{2,3},{3,0},{4,5},{5,6},{6,7},{7,4},{8,9},{9,10},{10,1... | collective-permute-start | bytes 393224 | tf_op jit(solution)/shard_map/cond/branch_1_fun/ppermute | solution.py:129
  24.9 0.7 %slice.28.kept = bf16[16,64,128]{2,1,0:T(8,128)(2,1)} slice(bf16[64,64,128]{2,1,0:T(8,128)(2,1)S(1)} %get-tuple-element.24), slice={[0:16], [0:64], [0:128]} | slice | bytes 524288 | tf_op jit(solution)/shard_map/cond/branch_1_fun/slice | solution.py:142
  25.6 2.2 %collective-permute-done.5.refs_2_ = bf16[8,64,128]{2,1,0:T(8,128)(2,1)S(1)} collective-permute-done((bf16[8,64,128]{2,1,0:T(8,128)(2,1)S(1)}, bf16[8,64,128]{2,1,0:T(8,128)(2,1)S(1)}, u32[]{:S(2)}, u32[]{:S(2)}) %collective-permute-start.5) | collective-permute-done | bytes 131104 | tf_op jit(solution)/shard_map/cond/branch_1_fun/ppermute | solution.py:129
  27.8 0.0 copy-start.6
  27.8 8.2 %collective-permute-done.4.refs_1_ = bf16[8,64,128]{2,1,0:T(8,128)(2,1)S(1)} collective-permute-done((bf16[8,64,128]{2,1,0:T(8,128)(2,1)S(1)}, bf16[8,64,128]{2,1,0:T(8,128)(2,1)S(1)}, u32[]{:S(2)}, u32[]{:S(2)}) %collective-permute-start.4) | collective-permute-done | bytes 131104 | tf_op jit(solution)/shard_map/cond/branch_1_fun/ppermute | solution.py:129
  36.0 0.0 copy-start.7
  36.0 0.0 collective-permute-done.3.refs_0_
  36.0 0.0 copy-start.8
  36.1 0.0 copy-done.6
  36.1 0.6 %copy-done.7 = bf16[8,64,128]{2,1,0:T(8,128)(2,1)} copy-done((bf16[8,64,128]{2,1,0:T(8,128)(2,1)}, bf16[8,64,128]{2,1,0:T(8,128)(2,1)S(1)}, u32[]{:S(2)}) %copy-start.7) | copy-done | bytes 131096 | tf_op jit(solution)/shard_map/cond
  36.7 0.1 copy-done.8
  36.7 1.3 %place.4 = bf16[64,2048]{1,0:T(8,128)(2,1)S(1)} custom-call(s32[17]{0:T(128)S(1)} %get-tuple-element.23.receive, bf16[16,64,128]{2,1,0:T(8,128)(2,1)} %slice.28.kept, bf16[8,64,128]{2,1,0:T(8,128)(2,1)} %copy-done.8, bf16[8,64,128]{2,1,0:T(8,128)(2,1)} %copy-done.7, bf16[8,64,128]{2,1,0:T(8,128)(2,1)} %copy-done.6), custom_call_target="tpu_custom_call" | custom-call | tf_op jit(solution)/shard_map/cond/branch_1_fun/place/pallas_call | solution.py:136
  38.0 0.0 copy-start.5
  38.1 0.7 %copy-done.5 = bf16[64,2048]{1,0:T(8,128)(2,1)} copy-done((bf16[64,2048]{1,0:T(8,128)(2,1)}, bf16[64,2048]{1,0:T(8,128)(2,1)S(1)}, u32[]{:S(2)}) %copy-start.5) | copy-done | bytes 262168
  (3 shorter events, 0.1 us)
Async XLA Ops:
  0.8 15.6 %copy-start = (bf16[64,2048]{1,0:T(8,128)(2,1)S(1)}, bf16[64,2048]{1,0:T(8,128)(2,1)}, u32[]{:S(2)}) copy-start(bf16[64,2048]{1,0:T(8,128)(2,1)} %query_ref.1) | copy-start | bytes 786436
  0.8 9.7 %collective-permute-start.11 = (bf16[64,512]{1,0:T(8,128)(2,1)S(1)}, bf16[64,512]{1,0:T(8,128)(2,1)S(1)}, u32[]{:S(2)}, u32[]{:S(2)}) collective-permute-start(bf16[64,512]{1,0:T(8,128)(2,1)S(1)} %pad_maximum_fusion.1), channel_id=1, source_target_pairs={{0,24},{4,28},{8,16},{12,20},{1,25},{5,29},{9,17},{13,21},{2,26},{... | collective-permute-start | bytes 196616 | tf_op jit(solution)/shard_map/ppermute | solution.py:174
  6.7 3.8 %collective-permute-start.10 = (bf16[64,512]{1,0:T(8,128)(2,1)S(1)}, bf16[64,512]{1,0:T(8,128)(2,1)S(1)}, u32[]{:S(2)}, u32[]{:S(2)}) collective-permute-start(bf16[64,512]{1,0:T(8,128)(2,1)S(1)} %pad_maximum_fusion.1), channel_id=1, source_target_pairs={{0,16},{4,20},{8,24},{12,28},{1,17},{5,21},{9,25},{13,29},{2,18},{... | collective-permute-start | bytes 196616 | tf_op jit(solution)/shard_map/ppermute | solution.py:174
  8.0 4.4 %collective-permute-start.9 = (bf16[64,512]{1,0:T(8,128)(2,1)S(1)}, bf16[64,512]{1,0:T(8,128)(2,1)S(1)}, u32[]{:S(2)}, u32[]{:S(2)}) collective-permute-start(bf16[64,512]{1,0:T(8,128)(2,1)S(1)} %pad_maximum_fusion.1), channel_id=1, source_target_pairs={{0,8},{4,12},{16,24},{20,28},{1,9},{5,13},{17,25},{21,29},{2,10},{... | collective-permute-start | bytes 196616 | tf_op jit(solution)/shard_map/ppermute | solution.py:174
  12.4 3.9 %collective-permute-start.12 = (bf16[256,512]{1,0:T(8,128)(2,1)S(1)}, bf16[256,512]{1,0:T(8,128)(2,1)S(1)}, u32[]{:S(2)}, u32[]{:S(2)}) collective-permute-start(bf16[256,512]{1,0:T(8,128)(2,1)S(1)} %pad_maximum_fusion.kv_own), channel_id=1, source_target_pairs={{0,4},{4,0},{8,12},{12,8},{16,20},{20,16},{24,28},{28,24},{1,5},{5... | collective-permute-start | bytes 786440 | tf_op jit(solution)/shard_map/ppermute | solution.py:176
  14.3 1.3 %copy-start.12 = (s32[64,8]{0,1:T(8,128)S(1)}, s32[64,8]{0,1:T(8,128)}, u32[]{:S(2)}) copy-start(s32[64,8]{0,1:T(8,128)} %param.12) | copy-start | bytes 6148
  15.6 0.7 %copy-start.13 = (s32[64,8]{0,1:T(8,128)S(1)}, s32[64,8]{0,1:T(8,128)}, u32[]{:S(2)}) copy-start(s32[64,8]{0,1:T(8,128)} %param.13) | copy-start | bytes 6148
  16.3 0.7 %copy-start.1 = (s32[17]{0:T(128)S(1)}, s32[17]{0:T(128)}, u32[]{:S(2)}) copy-start(s32[17]{0:T(128)} %get-tuple-element.31.send) | copy-start | bytes 208
  20.2 7.6 %collective-permute-start.5 = (bf16[8,64,128]{2,1,0:T(8,128)(2,1)S(1)}, bf16[8,64,128]{2,1,0:T(8,128)(2,1)S(1)}, u32[]{:S(2)}, u32[]{:S(2)}) collective-permute-start(bf16[8,64,128]{2,1,0:T(8,128)(2,1)S(1)} %get-tuple-element.37), channel_id=1, source_target_pairs={{0,3},{1,0},{2,1},{3,2},{4,7},{5,4},{6,5},{7,6},{8,11},{9,8},{10,9... | collective-permute-start | bytes 393224 | tf_op jit(solution)/shard_map/cond/branch_1_fun/ppermute | solution.py:129
  23.9 12.1 %collective-permute-start.4 = (bf16[8,64,128]{2,1,0:T(8,128)(2,1)S(1)}, bf16[8,64,128]{2,1,0:T(8,128)(2,1)S(1)}, u32[]{:S(2)}, u32[]{:S(2)}) collective-permute-start(bf16[8,64,128]{2,1,0:T(8,128)(2,1)S(1)} %get-tuple-element.38), channel_id=1, source_target_pairs={{0,2},{1,3},{2,0},{3,1},{4,6},{5,7},{6,4},{7,5},{8,10},{9,11},{10,... | collective-permute-start | bytes 393224 | tf_op jit(solution)/shard_map/cond/branch_1_fun/ppermute | solution.py:129
  23.9 12.1 %collective-permute-start.3 = (bf16[8,64,128]{2,1,0:T(8,128)(2,1)S(1)}, bf16[8,64,128]{2,1,0:T(8,128)(2,1)S(1)}, u32[]{:S(2)}, u32[]{:S(2)}) collective-permute-start(bf16[8,64,128]{2,1,0:T(8,128)(2,1)S(1)} %get-tuple-element.39), channel_id=1, source_target_pairs={{0,1},{1,2},{2,3},{3,0},{4,5},{5,6},{6,7},{7,4},{8,9},{9,10},{10,1... | collective-permute-start | bytes 393224 | tf_op jit(solution)/shard_map/cond/branch_1_fun/ppermute | solution.py:129
  27.8 8.2 %copy-start.6 = (bf16[8,64,128]{2,1,0:T(8,128)(2,1)}, bf16[8,64,128]{2,1,0:T(8,128)(2,1)S(1)}, u32[]{:S(2)}) copy-start(bf16[8,64,128]{2,1,0:T(8,128)(2,1)S(1)} %collective-permute-done.5.refs_2_) | copy-start | bytes 393220 | tf_op jit(solution)/shard_map/cond
  36.0 0.6 %copy-start.7 = (bf16[8,64,128]{2,1,0:T(8,128)(2,1)}, bf16[8,64,128]{2,1,0:T(8,128)(2,1)S(1)}, u32[]{:S(2)}) copy-start(bf16[8,64,128]{2,1,0:T(8,128)(2,1)S(1)} %collective-permute-done.4.refs_1_) | copy-start | bytes 393220 | tf_op jit(solution)/shard_map/cond
  36.0 0.7 %copy-start.8 = (bf16[8,64,128]{2,1,0:T(8,128)(2,1)}, bf16[8,64,128]{2,1,0:T(8,128)(2,1)S(1)}, u32[]{:S(2)}) copy-start(bf16[8,64,128]{2,1,0:T(8,128)(2,1)S(1)} %collective-permute-done.3.refs_0_) | copy-start | bytes 393220 | tf_op jit(solution)/shard_map/cond
  38.0 0.7 %copy-start.5 = (bf16[64,2048]{1,0:T(8,128)(2,1)}, bf16[64,2048]{1,0:T(8,128)(2,1)S(1)}, u32[]{:S(2)}) copy-start(bf16[64,2048]{1,0:T(8,128)(2,1)S(1)} %get-tuple-element.54) | copy-start | bytes 786436

commit v4 on v3

v4 whole, which is shorter than its diff:
```python
import functools
import math

import jax
import jax.numpy as jnp
from jax import lax
from jax.experimental import pallas as pl
from jax.experimental.pallas import tpu as pltpu
from jax.sharding import PartitionSpec as P

HD = 128
QH = 64
KVH = 8
BLK = 64
GROUP = QH // KVH
HEADS_AT_ONCE = 4
LANES = 128

floor_value = -1e30

SMEM = pl.BlockSpec(memory_space=pltpu.SMEM)
VMEM = pl.BlockSpec(memory_space=pltpu.VMEM)
ANY = pl.BlockSpec(memory_space=pl.ANY)
SMALL = 1024 * 1024


def shift_of(size):
    assert size & (size - 1) == 0
    return size.bit_length() - 1


def entry_bits(table, row):
    bits = jnp.int32(0)
    for entry in range(table.shape[0]):
        named = table[entry, row]
        bits = bits | jnp.where(named >= 0, jnp.int32(1) << jnp.maximum(named, 0), 0)
    return bits


def route_kernel(head_size, held, capacities, plan, vertical, slash, send, receive, level, counts):
    own = lax.axis_index("head")
    for pair in range(head_size * head_size):
        counts[pair] = 0
    largest = jnp.int32(0)
    for slot in range(plan.shape[0]):
        target = slot // held
        head = plan[slot]
        owner = head >> shift_of(held)
        pair = owner * head_size + target
        rank = counts[pair]
        counts[pair] = rank + 1
        largest = jnp.maximum(largest, jnp.where(owner == target, 0, rank + 1))
        place = ((target - owner) & (head_size - 1)) * held + rank
        send[jnp.where(owner == own, head & (held - 1), held)] = place
        receive[jnp.where(own == target, slot % held, held)] = place
    chosen = jnp.int32(0)
    for capacity in capacities[:-1]:
        chosen = chosen + (largest > capacity).astype(jnp.int32)
    level[0] = chosen
    for i in range(held):
        send[held + 1 + i] = entry_bits(vertical, own * held + i)
        send[2 * held + 1 + i] = entry_bits(slash, own * held + i)


def attention_kernel(seq_size, held, kv_heads, send, kv_own, kv_other, query_ref, out_ref):
    query_len = query_ref.shape[0]
    key_len = query_len
    own_seq = lax.axis_index("seq")
    chips = seq_size // 2
    half = chips * key_len

    piece = lax.broadcasted_iota(jnp.int32, (1, 2 * half), 1) // key_len
    core = jnp.where(piece < chips, own_seq & 1, 1 - (own_seq & 1))
    block = ((own_seq >> 1) ^ (piece & (chips - 1))) * 2 + core
    back = own_seq - block
    present = back >= 0
    back_shift = jnp.maximum(back, 0)
    row = lax.broadcasted_iota(jnp.int32, (query_len, LANES), 0)
    column = lax.broadcasted_iota(jnp.int32, (query_len, LANES), 1)
    causal = (column <= row) | (column >= key_len)
    score_scale = HD ** (-0.5) * math.log2(math.e)
    per_kv = held // kv_heads

    def scores_of(lead):
        heads = range(lead, min(lead + HEADS_AT_ONCE, held))
        key_at = lead // per_kv * HD
        key = jnp.concatenate([kv_own[:, key_at : key_at + HD], kv_other[:, key_at : key_at + HD]], axis=0)
        query = jnp.concatenate([query_ref[:, i * HD : (i + 1) * HD] for i in heads], axis=0)
        return lax.dot_general(
            query, key, (((1,), (1,)), ((), ())), preferred_element_type=jnp.float32
        )

    following = scores_of(0)
    for lead in range(0, held, HEADS_AT_ONCE):
        heads = range(lead, min(lead + HEADS_AT_ONCE, held))
        scores = following
        if lead + HEADS_AT_ONCE < held:
            following = scores_of(lead + HEADS_AT_ONCE)
        value_at = (lead // per_kv + kv_heads) * HD
        value = jnp.concatenate(
            [kv_own[:, value_at : value_at + HD], kv_other[:, value_at : value_at + HD]], axis=0
        )
        weights = []
        totals = []
        for at, i in enumerate(heads):
            hit = ((send[held + 1 + i] >> block) | (send[2 * held + 1 + i] >> back_shift)) & 1
            bias = jnp.where((hit == 1) & present, 0.0, floor_value)
            masked = scores[at * query_len : (at + 1) * query_len] + bias
            masked = jnp.concatenate(
                [jnp.where(causal, masked[:, :LANES], floor_value), masked[:, LANES:]], axis=1
            )
            row_max = jnp.max(masked, axis=1, keepdims=True)
            weight = jnp.exp2((masked - row_max) * score_scale)
            totals.append(1.0 / jnp.sum(weight, axis=1, keepdims=True))
            weights.append(weight.astype(jnp.bfloat16))
        mixture = jnp.dot(
            jnp.concatenate(weights, axis=0), value, preferred_element_type=jnp.float32
        )
        for at, i in enumerate(heads):
            mix = mixture[at * query_len : (at + 1) * query_len]
            out_ref[send[i]] = (mix * totals[at]).astype(out_ref.dtype)


def place_kernel(held, receive, packed, *refs):
    arrived = refs[:-2]
    out_ref, done = refs[-2:]
    slots = out_ref.shape[1] // HD
    for t in range(slots):
        place = receive[t]
        distance = place >> shift_of(held)
        rank = place & (held - 1)
        for d, ref in enumerate((packed,) + arrived):

            @pl.when(distance == d)
            def _(ref=ref):
                pltpu.make_async_copy(ref.at[rank], out_ref.at[:, pl.ds(t * HD, HD)], done.at[t]).start()

    for t in range(slots):
        pltpu.make_async_copy(packed.at[0], out_ref.at[:, pl.ds(t * HD, HD)], done.at[t]).wait()


def exchange(head_size, held, capacity, packed, receive):
    arrived = []
    for d in range(1, head_size):
        arrived.append(
            lax.ppermute(
                packed[d * held : d * held + capacity],
                "head",
                [(i, (i + d) % head_size) for i in range(head_size)],
            )
        )
    return pl.pallas_call(
        functools.partial(place_kernel, held),
        out_shape=jax.ShapeDtypeStruct((packed.shape[1], held * HD), packed.dtype),
        in_specs=[SMEM] + [ANY] * head_size,
        out_specs=ANY,
        scratch_shapes=[pltpu.SemaphoreType.DMA((held,))],
        compiler_params=pltpu.CompilerParams(vmem_limit_bytes=SMALL),
        name="place",
    )(receive, packed, *arrived)


def per_device(queries, keys, values, vertical, slash, plan):
    seq_size = lax.axis_size("seq")
    head_size = lax.axis_size("head")
    query_len = queries.shape[0]
    held = queries.shape[1] // HD
    kv_heads = max(1, held // GROUP)
    chips = seq_size // 2
    assert query_len == BLK and plan.shape[0] == held * head_size and chips & (chips - 1) == 0

    capacities = sorted({held * c // 16 for c in (5, 6, 7, 8, 16)} - {0})
    send, receive, level = pl.pallas_call(
        functools.partial(route_kernel, head_size, held, capacities),
        out_shape=[
            jax.ShapeDtypeStruct((3 * held + 1,), jnp.int32),
            jax.ShapeDtypeStruct((held + 1,), jnp.int32),
            jax.ShapeDtypeStruct((1,), jnp.int32),
        ],
        in_specs=[SMEM] * 3,
        out_specs=[SMEM] * 3,
        scratch_shapes=[pltpu.SMEM((head_size * head_size,), jnp.int32)],
        compiler_params=pltpu.CompilerParams(vmem_limit_bytes=SMALL),
        name="route",
    )(plan, vertical.T, slash.T)

    kv_at = lax.axis_index("head") * held // GROUP * HD
    kv = jnp.concatenate(
        [lax.dynamic_slice_in_dim(rows, kv_at, kv_heads * HD, axis=1) for rows in (keys, values)], axis=1
    )
    pieces = [kv]
    for m in range(1, chips):
        pairs = [(i, i ^ (2 * m)) for i in range(seq_size)]
        pieces.append(lax.ppermute(kv, "seq", pairs))
    kv_own = jnp.concatenate(pieces, axis=0)
    kv_other = lax.ppermute(kv_own, "seq", [(i, i ^ 1) for i in range(seq_size)])

    packed = pl.pallas_call(
        functools.partial(attention_kernel, seq_size, held, kv_heads),
        out_shape=jax.ShapeDtypeStruct((head_size * held, query_len, HD), jnp.bfloat16),
        in_specs=[SMEM] + [VMEM] * 3,
        out_specs=VMEM,
        compiler_params=pltpu.CompilerParams(vmem_limit_bytes=40 * 1024 * 1024),
        name="attention",
    )(send, kv_own, kv_other, queries)

    return lax.switch(
        level[0],
        [functools.partial(exchange, head_size, held, capacity) for capacity in capacities],
        packed,
        receive,
    )


def solution(mesh):
    in_specs = (P("seq", "head"), P("seq", None), P("seq", None), P(), P(), P())
    out_specs = P("seq", "head")
    return jax.shard_map(
        per_device, mesh=mesh, in_specs=in_specs, out_specs=out_specs, check_vma=False
    )
```

time: 39.1 us -> 29.7 us (0.76); the launches traced: 38.7 us -> 30.1 us
  starting transfers between devices: 14.4 us -> 9.33 us
  local copies, waits for them, and re-layouts: 4.33 us -> 2.16 us
  Pallas kernels: 6.21 us -> 4.95 us
  between operations: 1.42 us -> 0.73 us
  waiting for transfers between devices: 12.3 us -> 12.9 us
    ppermute x3, starting transfers between devices: 9.7 us -> 4.6 us  [per_device(): pieces.append(lax.ppermute(kv, 'seq', pairs))]
    ppermute x3, waiting for transfers between devices: 1.87 us -> 4.13 us  [per_device(): pieces.append(lax.ppermute(kv, 'seq', pairs))]
    pallas_call x1, Pallas kernels: 3.18 us -> 1.52 us  [per_device(): pl.pallas_call(functools.partial(attention_kernel, seq_size, held, kv_hea...]
    ppermute x3, waiting for transfers between devices: 10.4 us -> 8.77 us  [exchange(): lax.ppermute(packed[d * held:d * held + capacity], 'head', [(i, (i + d) %...]
    unnamed x12 -> x10, local copies, waits for them, and re-layouts: 2.11 us -> 1.36 us
    slice x1 -> x0, local copies, waits for them, and re-layouts: 0.72 us -> none  [exchange(): packed[:held]]
    cond x6 -> x0, local copies, waits for them, and re-layouts: 0.69 us -> none
    pallas_call x1, Pallas kernels: 1.75 us -> 2.32 us  [per_device(): pl.pallas_call(functools.partial(route_kernel, head_size, held, capacitie...]
  transfers between devices with their start and end apart: 7 -> 7, of which waited for: 3 -> 5; matrix products, arithmetic and copies ran while one was open for 2% -> 0% of each run, Pallas kernels for 5% -> 8%
where the time goes in v4:
time: 29.7 us; the launch traced here: 30.1 us
  waiting for transfers between devices  12.9 us (43%)
  starting transfers between devices  9.33 us (31%)
  Pallas kernels  4.95 us (17%)
  local copies, waits for them, and re-layouts  2.16 us (7%)
  between operations  0.73 us (2%)
    ppermute x3, waiting for transfers between devices, exchange(): lax.ppermute(packed[d * held:d * held + capacity], 'head', [(i, (i + d) %...  8.77 us
    ppermute x3, starting transfers between devices, exchange(): lax.ppermute(packed[d * held:d * held + capacity], 'head', [(i, (i + d) %...  4.66 us
    ppermute x3, starting transfers between devices, per_device(): pieces.append(lax.ppermute(kv, 'seq', pairs))  4.6 us
    ppermute x3, waiting for transfers between devices, per_device(): pieces.append(lax.ppermute(kv, 'seq', pairs))  4.13 us
    pallas_call x1, Pallas kernels, per_device(): pl.pallas_call(functools.partial(route_kernel, head_size, held, capacitie...  2.32 us
    pallas_call x1, Pallas kernels, per_device(): pl.pallas_call(functools.partial(attention_kernel, seq_size, held, kv_hea...  1.52 us
    unnamed x10, local copies, waits for them, and re-layouts  1.36 us
    pallas_call x1, Pallas kernels, exchange(): pl.pallas_call(functools.partial(place_kernel, held), out_shape=jax.Shape...  1.11 us
  transfers between devices with their start and end apart: 7, of which 5 were waited for; matrix products, arithmetic and copies ran while one was open for 0% of the time, Pallas kernels for 8%

profile of v4, /device:TPU:0, one launch (start us, length us, event | category | flops | bytes accessed | tf_op | source)
XLA Modules:
  0.0 30.1 jit_solution(8141933127858142148)
XLA Ops:
  0.0 0.8 %constant_dynamic-slice_fusion = (bf16[64,256]{1,0:T(8,128)(2,1)S(1)}, bf16[64,256]{1,0:T(8,128)(2,1)S(1)}) fusion(bf16[64,1024]{1,0:T(8,128)(2,1)} %param.13, s32[]{:T(128)S(6)} %select_n.10, bf16[64,1024]{1,0:T(8,128)(2,1)} %param.12), kind=kLoop, calls=%fused_computation.2 | loop fusion | bytes 131076 | tf_op jit(solution)/shard_map/dynamic_slice | solution.py:189
  0.8 0.0 copy-start
  0.8 4.0 %collective-permute-start.17 = (bf16[64,512]{1,0:T(8,128)(2,1)S(1)}, bf16[64,512]{1,0:T(8,128)(2,1)S(1)}, u32[]{:S(2)}, u32[]{:S(2)}) collective-permute-start(bf16[64,512]{1,0:T(8,128)(2,1)S(1)} %pad_maximum_fusion.1), channel_id=1, source_target_pairs={{0,24},{4,28},{8,16},{12,20},{16,8},{20,12},{24,0},{28,4},{1,25},{... | collective-permute-start | bytes 196616 | tf_op jit(solution)/shard_map/ppermute | solution.py:194
  4.8 0.5 %collective-permute-start.16 = (bf16[64,512]{1,0:T(8,128)(2,1)S(1)}, bf16[64,512]{1,0:T(8,128)(2,1)S(1)}, u32[]{:S(2)}, u32[]{:S(2)}) collective-permute-start(bf16[64,512]{1,0:T(8,128)(2,1)S(1)} %pad_maximum_fusion.1), channel_id=1, source_target_pairs={{0,16},{4,20},{8,24},{12,28},{16,0},{20,4},{24,8},{28,12},{1,17},{... | collective-permute-start | bytes 196616 | tf_op jit(solution)/shard_map/ppermute | solution.py:194
  5.3 0.1 collective-permute-start.15
  5.4 1.6 %collective-permute-done.17 = bf16[64,512]{1,0:T(8,128)(2,1)S(1)} collective-permute-done((bf16[64,512]{1,0:T(8,128)(2,1)S(1)}, bf16[64,512]{1,0:T(8,128)(2,1)S(1)}, u32[]{:S(2)}, u32[]{:S(2)}) %collective-permute-start.17) | collective-permute-done | bytes 65568 | tf_op jit(solution)/shard_map/ppermute | solution.py:194
  7.0 2.0 %collective-permute-done.16 = bf16[64,512]{1,0:T(8,128)(2,1)S(1)} collective-permute-done((bf16[64,512]{1,0:T(8,128)(2,1)S(1)}, bf16[64,512]{1,0:T(8,128)(2,1)S(1)}, u32[]{:S(2)}, u32[]{:S(2)}) %collective-permute-start.16) | collective-permute-done | bytes 65568 | tf_op jit(solution)/shard_map/ppermute | solution.py:194
  9.0 0.5 %collective-permute-done.15 = bf16[64,512]{1,0:T(8,128)(2,1)S(1)} collective-permute-done((bf16[64,512]{1,0:T(8,128)(2,1)S(1)}, bf16[64,512]{1,0:T(8,128)(2,1)S(1)}, u32[]{:S(2)}, u32[]{:S(2)}) %collective-permute-start.15) | collective-permute-done | bytes 65568 | tf_op jit(solution)/shard_map/ppermute | solution.py:194
  9.5 0.0 copy-start.1
  9.5 0.0 copy-start.2
  9.6 0.1 collective-permute-start.18
  9.6 0.0 copy-start.3
  9.7 0.6 %copy-done.1 = s32[64,8]{0,1:T(8,128)S(1)} copy-done((s32[64,8]{0,1:T(8,128)S(1)}, s32[64,8]{0,1:T(8,128)}, u32[]{:S(2)}) %copy-start.1) | copy-done | bytes 2072
  10.2 0.0 copy-done.2
  10.2 0.1 copy-done.3
  10.3 2.3 %route.1 = (s32[49]{0:T(128)S(1)}, s32[17]{0:T(128)S(1)}, s32[1]{0:T(128)}) custom-call(s32[64]{0:T(128)S(1)} %copy-done.3, s32[8,64]{1,0:T(8,128)S(1)} %bitcast.3, s32[8,64]{1,0:T(8,128)S(1)} %bitcast.4), custom_call_target="tpu_custom_call" | custom-call | tf_op jit(solution)/shard_map/route/pallas_call | solution.py:173
  13.3 0.0 collective-permute-done.18.kv_other
  13.3 0.0 copy-done
  13.3 1.5 %attention.1 = bf16[64,64,128]{2,1,0:T(8,128)(2,1)S(1)} custom-call(s32[49]{0:T(128)S(1)} %get-tuple-element.45.send, bf16[256,512]{1,0:T(8,128)(2,1)S(1)} %pad_maximum_fusion.kv_own, bf16[256,512]{1,0:T(8,128)(2,1)S(1)} %collective-permute-done.18.kv_other, bf16[64,2048]{1,0:T(8,128)(2,1)S(1)} %copy-done), custom_call_target="tpu_custom_call" | custom-call | tf_op jit(solution)/shard_map/attention/pallas_call | solution.py:198
  14.8 14.6 %conditional.1 = (bf16[64,2048]{1,0:T(8,128)(2,1)S(1)}) conditional(s32[]{:T(128)} %bitcast.2, (bf16[64,64,128]{2,1,0:T(8,128)(2,1)S(1)}, s32[17]{0:T(128)S(1)}) %tuple.20, (bf16[64,64,128]{2,1,0:T(8,128)(2,1)S(1)}, s32[17]{0:T(128)S(1)}) %tuple.20, (bf16[64,64,128]{2,1,0:T(8,128)(2,1)S(1)}, ...), branch_computations={%region_0.1_spmd, %region_1.2_spmd, %region_2.3_spmd, %region_3.4_... | conditional | bytes 4718720 | solution.py:207
  14.9 3.7 %collective-permute-start.5 = (bf16[6,64,128]{2,1,0:T(8,128)(2,1)S(1)}, bf16[6,64,128]{2,1,0:T(8,128)(2,1)S(1)}, u32[]{:S(2)}, u32[]{:S(2)}) collective-permute-start(bf16[6,64,128]{2,1,0:T(8,128)(2,1)S(1)} %get-tuple-element.51), channel_id=1, source_target_pairs={{0,3},{1,0},{2,1},{3,2},{4,7},{5,4},{6,5},{7,6},{8,11},{9,8},{10,9... | collective-permute-start | bytes 294920 | tf_op jit(solution)/shard_map/cond/branch_1_fun/ppermute | solution.py:146
  18.5 0.0 collective-permute-start.4
  18.5 1.0 %collective-permute-start.3 = (bf16[6,64,128]{2,1,0:T(8,128)(2,1)S(1)}, bf16[6,64,128]{2,1,0:T(8,128)(2,1)S(1)}, u32[]{:S(2)}, u32[]{:S(2)}) collective-permute-start(bf16[6,64,128]{2,1,0:T(8,128)(2,1)S(1)} %get-tuple-element.53), channel_id=1, source_target_pairs={{0,1},{1,2},{2,3},{3,0},{4,5},{5,6},{6,7},{7,4},{8,9},{9,10},{10,1... | collective-permute-start | bytes 294920 | tf_op jit(solution)/shard_map/cond/branch_1_fun/ppermute | solution.py:146
  19.5 2.1 %collective-permute-done.5.refs_2_ = bf16[6,64,128]{2,1,0:T(8,128)(2,1)S(1)} collective-permute-done((bf16[6,64,128]{2,1,0:T(8,128)(2,1)S(1)}, bf16[6,64,128]{2,1,0:T(8,128)(2,1)S(1)}, u32[]{:S(2)}, u32[]{:S(2)}) %collective-permute-start.5) | collective-permute-done | bytes 98336 | tf_op jit(solution)/shard_map/cond/branch_1_fun/ppermute | solution.py:146
  21.7 6.6 %collective-permute-done.4.refs_1_ = bf16[6,64,128]{2,1,0:T(8,128)(2,1)S(1)} collective-permute-done((bf16[6,64,128]{2,1,0:T(8,128)(2,1)S(1)}, bf16[6,64,128]{2,1,0:T(8,128)(2,1)S(1)}, u32[]{:S(2)}, u32[]{:S(2)}) %collective-permute-start.4) | collective-permute-done | bytes 98336 | tf_op jit(solution)/shard_map/cond/branch_1_fun/ppermute | solution.py:146
  28.3 0.0 collective-permute-done.3.refs_0_
  28.3 1.1 %place.6 = bf16[64,2048]{1,0:T(8,128)(2,1)S(1)} custom-call(s32[17]{0:T(128)S(1)} %get-tuple-element.32.receive, bf16[64,64,128]{2,1,0:T(8,128)(2,1)S(1)} %get-tuple-element.34.packed, bf16[6,64,128]{2,1,0:T(8,128)(2,1)S(1)} %collective-permute-done.3.refs_0_, bf16[6,64,128]{2,1,0:T(8,128)(2,1)S(1)} %collective-permute-done.4.refs_1_, ...), custom_call_target="tpu_custom_call" | custom-call | tf_op jit(solution)/shard_map/cond/branch_1_fun/place/pallas_call | solution.py:152
  29.4 0.0 copy-start.4
  29.5 0.7 %copy-done.4 = bf16[64,2048]{1,0:T(8,128)(2,1)} copy-done((bf16[64,2048]{1,0:T(8,128)(2,1)}, bf16[64,2048]{1,0:T(8,128)(2,1)S(1)}, u32[]{:S(2)}) %copy-start.4) | copy-done | bytes 262168
  (3 shorter events, 0.0 us)
Async XLA Ops:
  0.8 12.5 %copy-start = (bf16[64,2048]{1,0:T(8,128)(2,1)S(1)}, bf16[64,2048]{1,0:T(8,128)(2,1)}, u32[]{:S(2)}) copy-start(bf16[64,2048]{1,0:T(8,128)(2,1)} %query_ref.1) | copy-start | bytes 786436
  0.8 6.2 %collective-permute-start.17 = (bf16[64,512]{1,0:T(8,128)(2,1)S(1)}, bf16[64,512]{1,0:T(8,128)(2,1)S(1)}, u32[]{:S(2)}, u32[]{:S(2)}) collective-permute-start(bf16[64,512]{1,0:T(8,128)(2,1)S(1)} %pad_maximum_fusion.1), channel_id=1, source_target_pairs={{0,24},{4,28},{8,16},{12,20},{16,8},{20,12},{24,0},{28,4},{1,25},{... | collective-permute-start | bytes 196616 | tf_op jit(solution)/shard_map/ppermute | solution.py:194
  4.8 4.3 %collective-permute-start.16 = (bf16[64,512]{1,0:T(8,128)(2,1)S(1)}, bf16[64,512]{1,0:T(8,128)(2,1)S(1)}, u32[]{:S(2)}, u32[]{:S(2)}) collective-permute-start(bf16[64,512]{1,0:T(8,128)(2,1)S(1)} %pad_maximum_fusion.1), channel_id=1, source_target_pairs={{0,16},{4,20},{8,24},{12,28},{16,0},{20,4},{24,8},{28,12},{1,17},{... | collective-permute-start | bytes 196616 | tf_op jit(solution)/shard_map/ppermute | solution.py:194
  5.3 4.3 %collective-permute-start.15 = (bf16[64,512]{1,0:T(8,128)(2,1)S(1)}, bf16[64,512]{1,0:T(8,128)(2,1)S(1)}, u32[]{:S(2)}, u32[]{:S(2)}) collective-permute-start(bf16[64,512]{1,0:T(8,128)(2,1)S(1)} %pad_maximum_fusion.1), channel_id=1, source_target_pairs={{0,8},{4,12},{8,0},{12,4},{16,24},{20,28},{24,16},{28,20},{1,9},{5... | collective-permute-start | bytes 196616 | tf_op jit(solution)/shard_map/ppermute | solution.py:194
  9.5 0.7 %copy-start.1 = (s32[64,8]{0,1:T(8,128)S(1)}, s32[64,8]{0,1:T(8,128)}, u32[]{:S(2)}) copy-start(s32[64,8]{0,1:T(8,128)} %param.14) | copy-start | bytes 6148
  9.5 0.7 %copy-start.2 = (s32[64,8]{0,1:T(8,128)S(1)}, s32[64,8]{0,1:T(8,128)}, u32[]{:S(2)}) copy-start(s32[64,8]{0,1:T(8,128)} %param.15) | copy-start | bytes 6148
  9.6 3.7 %collective-permute-start.18 = (bf16[256,512]{1,0:T(8,128)(2,1)S(1)}, bf16[256,512]{1,0:T(8,128)(2,1)S(1)}, u32[]{:S(2)}, u32[]{:S(2)}) collective-permute-start(bf16[256,512]{1,0:T(8,128)(2,1)S(1)} %pad_maximum_fusion.kv_own), channel_id=1, source_target_pairs={{0,4},{4,0},{8,12},{12,8},{16,20},{20,16},{24,28},{28,24},{1,5},{5... | collective-permute-start | bytes 786440 | tf_op jit(solution)/shard_map/ppermute | solution.py:196
  9.6 0.7 %copy-start.3 = (s32[64]{0:T(128)S(1)}, s32[64]{0:T(128)}, u32[]{:S(2)}) copy-start(s32[64]{0:T(128)} %plan.1) | copy-start | bytes 772
  14.9 6.8 %collective-permute-start.5 = (bf16[6,64,128]{2,1,0:T(8,128)(2,1)S(1)}, bf16[6,64,128]{2,1,0:T(8,128)(2,1)S(1)}, u32[]{:S(2)}, u32[]{:S(2)}) collective-permute-start(bf16[6,64,128]{2,1,0:T(8,128)(2,1)S(1)} %get-tuple-element.51), channel_id=1, source_target_pairs={{0,3},{1,0},{2,1},{3,2},{4,7},{5,4},{6,5},{7,6},{8,11},{9,8},{10,9... | collective-permute-start | bytes 294920 | tf_op jit(solution)/shard_map/cond/branch_1_fun/ppermute | solution.py:146
  18.5 9.8 %collective-permute-start.4 = (bf16[6,64,128]{2,1,0:T(8,128)(2,1)S(1)}, bf16[6,64,128]{2,1,0:T(8,128)(2,1)S(1)}, u32[]{:S(2)}, u32[]{:S(2)}) collective-permute-start(bf16[6,64,128]{2,1,0:T(8,128)(2,1)S(1)} %get-tuple-element.52), channel_id=1, source_target_pairs={{0,2},{1,3},{2,0},{3,1},{4,6},{5,7},{6,4},{7,5},{8,10},{9,11},{10,... | collective-permute-start | bytes 294920 | tf_op jit(solution)/shard_map/cond/branch_1_fun/ppermute | solution.py:146
  18.5 9.8 %collective-permute-start.3 = (bf16[6,64,128]{2,1,0:T(8,128)(2,1)S(1)}, bf16[6,64,128]{2,1,0:T(8,128)(2,1)S(1)}, u32[]{:S(2)}, u32[]{:S(2)}) collective-permute-start(bf16[6,64,128]{2,1,0:T(8,128)(2,1)S(1)} %get-tuple-element.53), channel_id=1, source_target_pairs={{0,1},{1,2},{2,3},{3,0},{4,5},{5,6},{6,7},{7,4},{8,9},{9,10},{10,1... | collective-permute-start | bytes 294920 | tf_op jit(solution)/shard_map/cond/branch_1_fun/ppermute | solution.py:146
  29.4 0.7 %copy-start.4 = (bf16[64,2048]{1,0:T(8,128)(2,1)}, bf16[64,2048]{1,0:T(8,128)(2,1)S(1)}, u32[]{:S(2)}) copy-start(bf16[64,2048]{1,0:T(8,128)(2,1)S(1)} %get-tuple-element.90) | copy-start | bytes 786436
